TPU v7x, 32 devices: a whole 2x2x4 slice. The times are simulated.
32 devices in a mesh: grp: 2 (over x), gz: 8 (over z, y), col: 2 (over core).
Axes of the slice: x: 2, y: 2, z: 4, core: 2. Of those that a mesh axis runs over, the one named last changes fastest.
Arguments:
- noisy_image: float32 [4, 1024, 768], P('grp', 'gz', 'col'), parts along dimension 0, may hold values from -6 to 6
- fresh_noise: float32 [4, 1024, 768], P('grp', 'gz', 'col'), parts along dimension 0, may hold values from -6 to 6
- coil_maps: float32 [8, 4, 1024, 768], P('col', 'grp', 'gz'), parts along dimension 1, may hold values from -1.5 to 1.5
- measured: float32 [4, 768, 8, 1024], P('grp', 'gz', 'col'), parts along dimension 0, may hold values from -2.4 to 2.4
- sampled: int32 [768, 2048], P('gz', 'grp'), parts along dimension 1, may hold values 0 or 1
- first_kernel: bfloat16 [9, 64, 2], replicated, may hold values from -1.5 to 1.5
- inner_kernels: bfloat16 [1, 9, 64, 64], replicated, may hold values from -0.25 to 0.25
- last_kernel: bfloat16 [9, 2, 64], replicated, may hold values from -0.25 to 0.25
Outputs:
- next_image: float32 [4, 1024, 768], P('grp', 'gz', 'col'), parts along dimension 0
There are 2 independent parts, one for each index of `grp`. A program takes and returns all parts, laid end to end along the dimension named above; an argument that names none is the same for every part. Nothing has to cross between parts.
All inputs are finite; a program needn't handle non-finite values. No bound on the sum of `sampled` on one device may be relied on, other than what follows from the above.
Results may differ from a plain program's by a relative error of at most 0.00044.
Values may be sent and summed in bfloat16 or wider, within the bound.
A program may use at most 128 MiB of HBM per device.

v0:
```python
from functools import partial
import math

import jax
import jax.numpy as jnp
import numpy as np
from jax import lax
from jax.experimental import pallas as pl
from jax.experimental.pallas import tpu as pltpu
from jax.sharding import PartitionSpec as P

H_FAC = 8
W_FAC = 6
ROWS = 4


SCALE_NOW = 0.8
SIGMA_NOW = 0.6
STEP_GAIN = 1.0
SCALE_NEXT = 0.9
DIRECT_GAIN = 0.31622776601683794
NOISE_GAIN = 0.3


def with_halo(block, sides, width):
    for axis, dim in sides:
        count = lax.axis_size(axis)
        forward = [(i, i + 1) for i in range(count - 1)]
        backward = [(target, source) for source, target in forward]
        low = lax.ppermute(
            lax.slice_in_dim(block, block.shape[dim] - width, None, axis=dim), axis, forward
        )
        high = lax.ppermute(lax.slice_in_dim(block, 0, width, axis=dim), axis, backward)
        block = jnp.concatenate([low, block, high], axis=dim)
    return block


def row_banded(kernel, span):
    taps = kernel.reshape(3, 3, kernel.shape[1], kernel.shape[2])
    return jnp.stack(
        [
            jnp.pad(taps, ((start, span - 3 - start), (0, 0), (0, 0), (0, 0)))
            for start in range(span - 2)
        ]
    )


def network_kernel(
    groups,
    cols,
    tiles_ref,
    first_ref,
    inner_ref,
    last_ref,
    first_rows_ref,
    inner_rows_ref,
    inside_ref,
    out_ref,
    first_held,
    inner_held,
):
    frame, width = inside_ref.shape
    half = width // 2

    def act(halved, keep):
        return (halved + halved * jnp.tanh(halved)) * (inside_ref[...] * keep)

    def first_layer(group):
        halved = jnp.dot(
            tiles_ref[group // ROWS],
            first_ref[lax.rem(group, ROWS)],
            preferred_element_type=jnp.float32,
        )
        hidden = act(halved, first_rows_ref[group])
        slot = lax.rem(group, ROWS)
        first_held[slot, 0] = pltpu.roll(hidden, 1, 0).astype(jnp.bfloat16)
        first_held[slot, 1] = hidden.astype(jnp.bfloat16)
        first_held[slot, 2] = pltpu.roll(hidden, frame - 1, 0).astype(jnp.bfloat16)

    def inner_layer(group):
        slot = lax.rem(group, ROWS)
        after = lax.rem(group + 1, ROWS)
        total = None
        for shift in range(3):
            part = jnp.dot(
                first_held[slot, shift],
                inner_ref[shift, :width],
                preferred_element_type=jnp.float32,
            ) + jnp.dot(
                first_held[after, shift, :, :half],
                inner_ref[shift, width:],
                preferred_element_type=jnp.float32,
            )
            total = part if total is None else total + part
        inner_held[slot] = act(total, inner_rows_ref[group]).astype(jnp.bfloat16)

    def last_layer(group):
        slot = lax.rem(group, ROWS)
        after = lax.rem(group + 1, ROWS)
        lanes = (((1,), (1,)), ((), ()))
        part = lax.dot_general(
            last_ref[:, :width], inner_held[slot], lanes, preferred_element_type=jnp.float32
        ) + lax.dot_general(
            last_ref[:, width:],
            inner_held[after, :, :half],
            lanes,
            preferred_element_type=jnp.float32,
        )
        left = part[:8]
        left = jnp.concatenate([left[:, frame - 1 :], left[:, : cols - 1]], axis=1)
        out_ref[group] = left + part[8:16, :cols] + part[16:24, 1 : cols + 1]

    for group in range(4):
        first_layer(group)
    for group in range(2):
        inner_layer(group)

    def step(group, carry):
        last_layer(group)
        inner_layer(group + 2)
        first_layer(group + 4)
        return carry

    lax.fori_loop(0, groups, step, 0)


def network(image, first_kernel, inner_kernels, last_kernel):
    channels, rows, cols = image.shape
    hidden = first_kernel.shape[1]
    groups = rows // ROWS
    frame = cols + 16
    width = ROWS * hidden
    span = ROWS * ROWS + 2
    tile_count = groups // ROWS + 1
    padded = with_halo(image.astype(jnp.bfloat16), (("gz", 1), ("col", 2)), 3)
    padded = jnp.pad(padded, ((0, 0), (0, ROWS * ROWS * tile_count + 2 - rows - 6), (0, 0)))
    gap = jnp.zeros(padded.shape[:2] + (frame - cols - 6,), padded.dtype)
    ring = jnp.concatenate([padded[:, :, 3:], gap, padded[:, :, :3]], axis=2)
    shifted = jnp.stack([jnp.roll(ring, 1 - shift, axis=2) for shift in range(3)])
    tiles = jnp.stack(
        [shifted[:, :, ROWS * ROWS * t : ROWS * ROWS * t + span] for t in range(tile_count)]
    )
    depth = 3 * channels * span
    tiles = jnp.transpose(tiles.reshape(tile_count, depth, frame), (0, 2, 1))
    tiles = jnp.pad(tiles, ((0, 0), (0, 0), (0, 128 - depth)))
    half = jnp.asarray(0.5, jnp.bfloat16)
    first = jnp.transpose(row_banded(first_kernel * half, span), (2, 4, 1, 0, 3))
    first = first.reshape(depth, ROWS, width)
    first = jnp.pad(jnp.transpose(first, (1, 0, 2)), ((0, 0), (0, 128 - depth), (0, 0)))
    inner = jnp.transpose(row_banded(inner_kernels[0] * half, ROWS + 2), (2, 1, 4, 0, 3))
    inner = inner.reshape(3, (ROWS + 2) * hidden, width)
    last = jnp.transpose(row_banded(last_kernel, ROWS + 2), (2, 0, 3, 1, 4))
    last = last.reshape(3 * ROWS * channels, (ROWS + 2) * hidden)
    last = jnp.pad(last, ((0, 32 - last.shape[0]), (0, 0)))
    top = lax.axis_index("gz") * rows
    height = rows * lax.axis_size("gz")
    across = cols * lax.axis_size("col")

    def row_mask(count, offset):
        place = top + ROWS * jnp.arange(count)[:, None] + jnp.arange(ROWS)[None, :] - offset
        keep = ((place >= 0) & (place < height)).astype(jnp.float32)
        return jnp.repeat(keep, hidden, axis=1).reshape(count, 1, width)

    spot = jnp.arange(frame)
    spot = jnp.where(spot < cols + 8, spot, spot - frame) + lax.axis_index("col") * cols
    inside = ((spot >= 0) & (spot < across)).astype(jnp.float32)
    inside = jnp.broadcast_to(inside[:, None], (frame, width))
    result = pl.pallas_call(
        partial(network_kernel, groups, cols),
        out_shape=jax.ShapeDtypeStruct((groups, ROWS * channels, cols), jnp.float32),
        in_specs=[pl.BlockSpec(memory_space=pltpu.VMEM)] * 7,
        out_specs=pl.BlockSpec(memory_space=pltpu.VMEM),
        scratch_shapes=[
            pltpu.VMEM((ROWS, 3, frame, width), jnp.bfloat16),
            pltpu.VMEM((ROWS, frame, width), jnp.bfloat16),
        ],
        compiler_params=pltpu.CompilerParams(vmem_limit_bytes=40 * 1024 * 1024),
        name="network",
    )(tiles, first, inner, last, row_mask(groups + 4, 2), row_mask(groups + 2, 1), inside)
    result = result.reshape(groups, ROWS, channels, cols)
    return jnp.transpose(result, (2, 0, 1, 3)).reshape(channels, rows, cols)


def rotation(rows_len, cols_len, modulus, direction):
    first_index = jnp.arange(rows_len, dtype=jnp.int32)
    second_index = jnp.arange(cols_len, dtype=jnp.int32)
    phase_index = first_index[:, None] * second_index[None, :] % modulus
    angles = phase_index.astype(jnp.float32) * (direction * 2.0 * math.pi / modulus)
    return (jnp.cos(angles), jnp.sin(angles))


def complex_dot(matrix_pair, data_pair, contracting):
    product = partial(
        lax.dot_general,
        dimension_numbers=(contracting, ((), ())),
        precision=lax.Precision.HIGH,
        preferred_element_type=jnp.float32,
    )
    return (
        product(matrix_pair[0], data_pair[0]) - product(matrix_pair[1], data_pair[1]),
        product(matrix_pair[0], data_pair[1]) + product(matrix_pair[1], data_pair[0]),
    )


def complex_mul(first_pair, second_pair):
    return (
        first_pair[0] * second_pair[0] - first_pair[1] * second_pair[1],
        first_pair[0] * second_pair[1] + first_pair[1] * second_pair[0],
    )


def transform_last(data_pair, outer_len, direction):
    vectors, length = data_pair[0].shape
    inner_len = length // outer_len
    shaped = (
        data_pair[0].reshape(vectors, outer_len, inner_len),
        data_pair[1].reshape(vectors, outer_len, inner_len),
    )
    sectioned = complex_dot(
        rotation(outer_len, outer_len, outer_len, direction), shaped, ((1,), (1,))
    )
    twiddles = rotation(outer_len, inner_len, length, direction)
    twisted = complex_mul(sectioned, (twiddles[0][:, None, :], twiddles[1][:, None, :]))
    finished = complex_dot(
        rotation(inner_len, inner_len, inner_len, direction), twisted, ((1,), (2,))
    )
    factor = 1.0 / math.sqrt(length)
    return (
        finished[0].reshape(length, vectors) * factor,
        finished[1].reshape(length, vectors) * factor,
    )


def transform_first(data_pair, outer_len, direction):
    length, vectors = data_pair[0].shape
    inner_len = length // outer_len
    shaped = (
        data_pair[0].reshape(outer_len, inner_len, vectors),
        data_pair[1].reshape(outer_len, inner_len, vectors),
    )
    sectioned = complex_dot(
        rotation(outer_len, outer_len, outer_len, direction), shaped, ((1,), (0,))
    )
    twiddles = rotation(outer_len, inner_len, length, direction)
    twisted = complex_mul(sectioned, (twiddles[0][:, :, None], twiddles[1][:, :, None]))
    finished = complex_dot(
        rotation(inner_len, inner_len, inner_len, direction), twisted, ((1,), (1,))
    )
    factor = 1.0 / math.sqrt(length)
    return (
        finished[0].reshape(length, vectors) * factor,
        finished[1].reshape(length, vectors) * factor,
    )


def split_pair(real, imag, axis):
    both = jnp.concatenate([real, imag], axis=axis)
    high = both.astype(jnp.bfloat16)
    low = (both - high.astype(jnp.float32)).astype(jnp.bfloat16)
    return jnp.concatenate([high, low, high], axis=axis)


def pair_matrix(inner, length, transposed):
    angles = np.outer(np.arange(inner), np.arange(inner)) % inner * (2.0 * np.pi / inner)
    cosines, sines = np.cos(angles), np.sin(angles)
    matrix = np.block([[cosines, sines], [-sines, cosines]]) / np.sqrt(length)
    if transposed:
        matrix = matrix.T
    high = matrix.astype(jnp.bfloat16)
    low = (matrix - high.astype(np.float64)).astype(jnp.bfloat16)
    return high, low


def twiddle_rows(outer, inner):
    angles = np.outer(np.arange(outer), np.arange(inner)) * (2.0 * np.pi / (outer * inner))
    return np.stack([np.cos(angles), np.sin(angles)], axis=1).astype(np.float32)


def turn(pair, twiddle_ref, index, sign):
    if index == 0:
        return pair
    cosine = twiddle_ref[index, 0:1]
    sine = sign * twiddle_ref[index, 1:2]
    return (pair[0] * cosine - pair[1] * sine, pair[0] * sine + pair[1] * cosine)


def level_out(out_ref, body_rows):
    values = out_ref[:, :body_rows, :]
    top = jnp.max(jnp.max(jnp.abs(values), axis=0), axis=0, keepdims=True)
    top = jnp.maximum(jnp.max(top, axis=1, keepdims=True), 1e-30)
    power = jnp.ceil(jnp.log2(top)) - 13.0
    out_ref[:, :body_rows, :] = values * jnp.exp2(-power)
    tail = out_ref.shape[1] - body_rows
    out_ref[:, body_rows:, :] = jnp.broadcast_to(
        power[None], (out_ref.shape[0], tail, out_ref.shape[2])
    )


def columns_kernel(clean_ref, maps_ref, matrix_ref, twiddle_ref, out_ref):
    coils, _, rows, full = maps_ref.shape
    groups = out_ref.shape[0]
    inner = full // 3
    piece = inner // groups
    root = math.sqrt(0.75)
    clean = (clean_ref[0], clean_ref[1])
    for start in range(0, coils, 2):
        image = [
            complex_mul((maps_ref[coil, 0], maps_ref[coil, 1]), clean)
            for coil in (start, start + 1)
        ]
        image = [jnp.concatenate([image[0][part], image[1][part]], axis=0) for part in range(2)]
        first, second, third = [
            (image[0][:, n * inner : (n + 1) * inner], image[1][:, n * inner : (n + 1) * inner])
            for n in range(3)
        ]
        total = (second[0] + third[0], second[1] + third[1])
        apart = (root * (second[0] - third[0]), root * (second[1] - third[1]))
        middle = (first[0] - 0.5 * total[0], first[1] - 0.5 * total[1])
        bins = (
            (first[0] + total[0], first[1] + total[1]),
            (middle[0] + apart[1], middle[1] - apart[0]),
            (middle[0] - apart[1], middle[1] + apart[0]),
        )
        for index in range(3):
            turned = turn(bins[index], twiddle_ref, index, -1.0)
            result = lax.dot_general(
                matrix_ref[...],
                split_pair(turned[0], turned[1], 1),
                (((1,), (1,)), ((), ())),
                preferred_element_type=jnp.float32,
            )
            for part in range(2):
                for which in range(2):
                    base = ((part * coils + start + which) * 3 + index) * piece
                    block = result[part * inner : (part + 1) * inner]
                    block = block[:, which * rows : (which + 1) * rows]
                    out_ref[:, base : base + piece, :] = block.reshape(groups, piece, rows)
    level_out(out_ref, 2 * coils * 3 * piece)


def rows_kernel(
    arrived_ref, measured_ref, keep_ref, forward_ref, inverse_ref, twiddle_ref, out_ref
):
    groups, _, rows = arrived_ref.shape
    vectors = measured_ref.shape[1]
    height = groups * rows
    inner = height // 4
    copies = vectors // keep_ref.shape[0]
    scales = [jnp.exp2(arrived_ref[g, 2 * vectors : 2 * vectors + 1, :]) for g in range(groups)]
    whole = [
        jnp.concatenate(
            [
                arrived_ref[g, part * vectors : (part + 1) * vectors, :] * scales[g]
                for g in range(groups)
            ],
            axis=1,
        )
        for part in range(2)
    ]
    a0, a1, a2, a3 = [
        (whole[0][:, n * inner : (n + 1) * inner], whole[1][:, n * inner : (n + 1) * inner])
        for n in range(4)
    ]
    even = (a0[0] + a2[0], a0[1] + a2[1])
    odd = (a0[0] - a2[0], a0[1] - a2[1])
    even_next = (a1[0] + a3[0], a1[1] + a3[1])
    odd_next = (a1[0] - a3[0], a1[1] - a3[1])
    bins = (
        (even[0] + even_next[0], even[1] + even_next[1]),
        (odd[0] + odd_next[1], odd[1] - odd_next[0]),
        (even[0] - even_next[0], even[1] - even_next[1]),
        (odd[0] - odd_next[1], odd[1] + odd_next[0]),
    )
    turned_back = []
    for index in range(4):
        turned = turn(bins[index], twiddle_ref, index, -1.0)
        spectrum = jnp.dot(
            split_pair(turned[0], turned[1], 1),
            forward_ref[...],
            preferred_element_type=jnp.float32,
        )
        lanes = slice(index * inner, (index + 1) * inner)
        keep = jnp.concatenate([keep_ref[:, lanes]] * copies, axis=0)
        residual = [
            keep * (spectrum[:, part * inner : (part + 1) * inner] - measured_ref[part, :, lanes])
            for part in range(2)
        ]
        inverse = jnp.dot(
            split_pair(residual[0], residual[1], 1),
            inverse_ref[...],
            preferred_element_type=jnp.float32,
        )
        turned_back.append(turn((inverse[:, :inner], inverse[:, inner:]), twiddle_ref, index, 1.0))
    c0, c1, c2, c3 = turned_back
    even = (c0[0] + c2[0], c0[1] + c2[1])
    odd = (c0[0] - c2[0], c0[1] - c2[1])
    even_next = (c1[0] + c3[0], c1[1] + c3[1])
    odd_next = (c1[0] - c3[0], c1[1] - c3[1])
    blocks = (
        (even[0] + even_next[0], even[1] + even_next[1]),
        (odd[0] - odd_next[1], odd[1] + odd_next[0]),
        (even[0] - even_next[0], even[1] - even_next[1]),
        (odd[0] + odd_next[1], odd[1] - odd_next[0]),
    )
    per_block = inner // rows
    for g in range(groups):
        lanes = slice((g % per_block) * rows, (g % per_block + 1) * rows)
        for part in range(2):
            out_ref[g, part * vectors : (part + 1) * vectors, :] = blocks[g // per_block][part][
                :, lanes
            ]
    level_out(out_ref, 2 * vectors)


def combine_kernel(arrived_ref, maps_ref, matrix_ref, twiddle_ref, out_ref):
    coils, _, rows, full = maps_ref.shape
    groups = arrived_ref.shape[0]
    inner = full // 3
    piece = inner // groups
    body_rows = 2 * coils * 3 * piece
    root = math.sqrt(0.75)
    scales = [jnp.exp2(arrived_ref[g, body_rows : body_rows + 1, :]) for g in range(groups)]

    def plane(part, coil, index):
        base = ((part * coils + coil) * 3 + index) * piece
        return jnp.concatenate(
            [arrived_ref[g, base : base + piece, :] * scales[g] for g in range(groups)], axis=0
        )

    turned = []
    for index in range(3):
        parts = [
            jnp.concatenate([plane(part, coil, index) for coil in range(coils)], axis=1)
            for part in range(2)
        ]
        result = lax.dot_general(
            split_pair(parts[0], parts[1], 0),
            matrix_ref[...],
            (((0,), (0,)), ((), ())),
            preferred_element_type=jnp.float32,
        )
        turned.append(turn((result[:, :inner], result[:, inner:]), twiddle_ref, index, 1.0))
    c0, c1, c2 = turned
    total = (c1[0] + c2[0], c1[1] + c2[1])
    apart = (root * (c1[0] - c2[0]), root * (c1[1] - c2[1]))
    middle = (c0[0] - 0.5 * total[0], c0[1] - 0.5 * total[1])
    blocks = (
        (c0[0] + total[0], c0[1] + total[1]),
        (middle[0] - apart[1], middle[1] + apart[0]),
        (middle[0] + apart[1], middle[1] - apart[0]),
    )
    for n in range(3):
        lanes = slice(n * inner, (n + 1) * inner)
        real = imag = None
        for coil in range(coils):
            back = [blocks[n][part][coil * rows : (coil + 1) * rows] for part in range(2)]
            map_real = maps_ref[coil, 0, :, lanes]
            map_imag = maps_ref[coil, 1, :, lanes]
            term_real = map_real * back[0] + map_imag * back[1]
            term_imag = map_real * back[1] - map_imag * back[0]
            real = term_real if real is None else real + term_real
            imag = term_imag if imag is None else imag + term_imag
        out_ref[0, :, lanes] = real
        out_ref[1, :, lanes] = imag


def call_whole(kernel, shape, name, *operands):
    return pl.pallas_call(
        kernel,
        out_shape=jax.ShapeDtypeStruct(shape, jnp.float32),
        in_specs=[pl.BlockSpec(memory_space=pltpu.VMEM)] * len(operands),
        out_specs=pl.BlockSpec(memory_space=pltpu.VMEM),
        compiler_params=pltpu.CompilerParams(vmem_limit_bytes=50 * 1024 * 1024),
        name=name,
    )(*operands)


def exchange(values):
    moved = lax.all_to_all(
        values.astype(jnp.float16), "gz", split_axis=0, concat_axis=0, tiled=True
    )
    return moved.astype(jnp.float32)


def aligned_gradient(clean_wide, coil_maps, measured, sampled):
    coils, _, rows, full = coil_maps.shape
    groups = lax.axis_size("gz")
    height = rows * groups
    inner = full // 3
    piece = inner // groups
    vectors = coils * 3 * piece
    sent = (groups, 2 * vectors + 16, rows)
    high, low = pair_matrix(inner, full, False)
    left = np.concatenate([high, high, low], axis=1)
    right = np.concatenate([high, high, low], axis=0)
    columns_twiddles = twiddle_rows(3, inner)
    spectra = call_whole(
        columns_kernel, sent, "columns", clean_wide, coil_maps, left, columns_twiddles
    )
    measured, sampled, spectra = lax.optimization_barrier((measured, sampled, spectra))
    arrived = exchange(spectra)
    place = jnp.arange(height)
    source = place // (height // 4) + 4 * (place % (height // 4))
    permute = (place[:, None] == source[None, :]).astype(jnp.float32)
    targets = jnp.transpose(measured.reshape(2, piece, 3, coils, height), (0, 3, 2, 1, 4))
    targets = jnp.dot(
        targets.reshape(2 * vectors, height), permute, precision=lax.Precision.HIGH
    ).reshape(2, vectors, height)
    keep = jnp.transpose(sampled.reshape(piece, 3, height), (1, 0, 2)).astype(jnp.bfloat16)
    keep = jnp.dot(
        keep.reshape(3 * piece, height),
        permute.astype(jnp.bfloat16),
        preferred_element_type=jnp.float32,
    )
    rows_high, rows_low = pair_matrix(height // 4, height, True)
    back_high, back_low = pair_matrix(height // 4, height, False)
    residual = call_whole(
        rows_kernel,
        sent,
        "rows",
        arrived,
        targets,
        keep,
        np.concatenate([rows_high, rows_high, rows_low], axis=0),
        np.concatenate([back_high, back_high, back_low], axis=0),
        twiddle_rows(4, height // 4),
    )
    arrived = exchange(residual)
    return call_whole(
        combine_kernel, (2, rows, full), "combine", arrived, coil_maps, right, columns_twiddles
    )


def gradient(clean_wide, coil_maps, measured, sampled):
    coils, _, rows, full = coil_maps.shape
    groups = lax.axis_size("gz")
    whole = rows % 128 == 0 and coils % 2 == 0 and full % 768 == 0
    if whole and (rows * groups) % 1024 == 0 and full % (48 * groups) == 0:
        return aligned_gradient(clean_wide, coil_maps, measured, sampled)
    return plain_gradient(clean_wide, coil_maps, measured, sampled)


def plain_gradient(clean_wide, coil_maps, measured, sampled):
    maps_real = coil_maps[:, 0]
    maps_imag = coil_maps[:, 1]
    coil_count, row_count, full_cols = maps_real.shape
    coil_pair = complex_mul((maps_real, maps_imag), (clean_wide[0][None], clean_wide[1][None]))
    spectra = transform_last(
        (
            coil_pair[0].reshape(coil_count * row_count, full_cols),
            coil_pair[1].reshape(coil_count * row_count, full_cols),
        ),
        W_FAC,
        -1.0,
    )
    groups = lax.axis_size("gz")
    pencil = full_cols // groups
    arrived = (
        lax.all_to_all(
            spectra[0].reshape(groups, pencil, coil_count, row_count),
            "gz",
            split_axis=0,
            concat_axis=3,
            tiled=True,
        ),
        lax.all_to_all(
            spectra[1].reshape(groups, pencil, coil_count, row_count),
            "gz",
            split_axis=0,
            concat_axis=3,
            tiled=True,
        ),
    )
    item_count = arrived[0].shape[2]
    height = arrived[0].shape[3]
    flattened = (
        arrived[0].reshape(pencil * item_count, height),
        arrived[1].reshape(pencil * item_count, height),
    )
    transformed = transform_last(flattened, H_FAC, -1.0)
    keeping = sampled.astype(jnp.float32)[:, None, :]
    resid_real = keeping * (transformed[0].T.reshape(pencil, item_count, height) - measured[0])
    resid_imag = keeping * (transformed[1].T.reshape(pencil, item_count, height) - measured[1])
    height = resid_real.shape[2]
    inverse = transform_last(
        (
            resid_real.reshape(pencil * coil_count, height),
            resid_imag.reshape(pencil * coil_count, height),
        ),
        H_FAC,
        1.0,
    )
    arrived = (
        lax.all_to_all(
            inverse[0].T.reshape(pencil, coil_count, groups, row_count),
            "gz",
            split_axis=2,
            concat_axis=0,
            tiled=True,
        ),
        lax.all_to_all(
            inverse[1].T.reshape(pencil, coil_count, groups, row_count),
            "gz",
            split_axis=2,
            concat_axis=0,
            tiled=True,
        ),
    )
    item_count = arrived[0].shape[1]
    flattened = (
        arrived[0].reshape(full_cols, item_count * row_count),
        arrived[1].reshape(full_cols, item_count * row_count),
    )
    transformed = transform_first(flattened, W_FAC, 1.0)
    back_real = jnp.transpose(transformed[0].reshape(full_cols, item_count, row_count), (1, 2, 0))
    back_imag = jnp.transpose(transformed[1].reshape(full_cols, item_count, row_count), (1, 2, 0))
    grad_real = jnp.sum(maps_real * back_real + maps_imag * back_imag, axis=0)
    grad_imag = jnp.sum(maps_real * back_imag - maps_imag * back_real, axis=0)
    return jnp.stack([grad_real, grad_imag])


def local(
    noisy_image, fresh_noise, coil_maps, measured, sampled, first_kernel, inner_kernels, last_kernel
):
    predicted = network(noisy_image, first_kernel, inner_kernels, last_kernel)
    clean = (noisy_image - SIGMA_NOW * predicted) / SCALE_NOW
    clean_wide = lax.all_gather(clean, "col", axis=2, tiled=True)
    grad = gradient(clean_wide, coil_maps, measured, sampled)
    grad_tile = lax.psum_scatter(
        grad, "col", scatter_dimension=2, tiled=True
    )
    update = clean - STEP_GAIN * grad_tile
    return SCALE_NEXT * update + DIRECT_GAIN * predicted + NOISE_GAIN * fresh_noise


def solution(mesh):
    in_specs = (
        P("grp", "gz", "col"),
        P("grp", "gz", "col"),
        P("col", "grp", "gz", None),
        P("grp", "gz", "col", None),
        P("gz", "grp"),
        P(),
        P(),
        P(),
    )
    out_specs = P("grp", "gz", "col")
    return jax.shard_map(local, mesh=mesh, in_specs=in_specs, out_specs=out_specs, check_vma=False)
```

profile of v0, /device:TPU:0, one launch (start us, length us, event | category | flops | bytes accessed | tf_op | source)
XLA Modules:
  0.0 195.7 jit_solution(14642255362709156408)
XLA Ops:
  6.5 1.0 convert_element_type.99
  7.6 4.9 %collective-permute-start = (bf16[2,3,384]{2,1,0:T(4,128)(2,1)S(1)}, bf16[2,3,384]{2,1,0:T(4,128)(2,1)S(1)}, u32[]{:S(2)}, u32[]{:S(2)}) collective-permute-start(bf16[2,3,384]{2,1,0:T(4,128)(2,1)S(1)} %get-tuple-element.28), channel_id=1, source_target_pairs={{0,2},{2,4},{4,6},{6,8},{8,10},{10,12},{12,14},{1,3},{3,5},{5,7},{... | collective-permute-start | bytes 13832 | tf_op jit(solution)/shard_map/ppermute | solution.py:30
  12.5 1.3 collective-permute-start.1
  13.8 0.7 broadcast_multiply_fusion.3
  14.5 0.7 copy.102
  15.2 0.9 broadcast_multiply_fusion.2
  16.9 0.3 maximum_bitcast_fusion
  17.2 0.7 collective-permute-done.1
  18.1 1.3 collective-permute-start.2
  19.4 1.3 collective-permute-start.3
  21.9 0.8 copy.101
  22.8 0.7 reshape.111.inner_ref
  27.2 25.7 %network.1 = f32[32,8,384]{2,1,0:T(8,128)S(1)} custom-call(bf16[9,400,128]{2,1,0:T(8,128)(2,1)S(1)} %pad.113.tiles_ref, bf16[4,128,256]{2,1,0:T(8,128)(2,1)S(1)} %pad.130.first_ref, bf16[3,384,256]{2,1,0:T(8,128)(2,1)S(1)} %reshape.111.inner_ref, bf16[32,384]{1,0:T(8,128)(2,1)S(1)} %pad.139.last_ref, f32[36,1,256]{2,1,0:T(1,128)S(1)} %reshape_reshape.6.first_rows_ref, ...), custom_call_target="tpu_custom_call" | custom-call | tf_op jit(solution)/shard_map/network/pallas_call | solution.py:168
  52.9 0.8 broadcast_multiply_fusion.1
  54.3 3.2 %all_gather.3.clean_ref = f32[2,128,768]{2,1,0:T(8,128)S(1)} all-gather(f32[2,128,384]{2,1,0:T(8,128)S(1)} %subtract_multiply_fusion), channel_id=1, replica_groups=mesh['grp'=2,'gz'=8,'col'=2] {'col'}, dimensions={2}, use_global_device_ids=true | all-gather | bytes 1179648 | tf_op jit(solution)/shard_map/all_gather | solution.py:627
  57.6 7.0 %columns.1 = f32[8,784,128]{2,1,0:T(8,128)} custom-call(f32[2,128,768]{2,1,0:T(8,128)S(1)} %all_gather.3.clean_ref, f32[4,2,128,768]{3,2,1,0:T(8,128)} %maps_ref.3, bf16[512,1536]{1,0:T(8,128)(2,1)S(1)} %copy-done.3, f32[3,2,256]{2,1,0:T(2,128)S(1)} %copy-done.4), custom_call_target="tpu_custom_call" | custom-call | tf_op jit(solution)/shard_map/columns/pallas_call | solution.py:468
  64.6 3.4 %convert_element_type.103 = f16[8,784,128]{2,1,0:T(8,128)(2,1)} convert(f32[8,784,128]{2,1,0:T(8,128)} %columns.1) | non-fusion elementwise | flops 802816 | bytes 4816896 | tf_op jit(solution)/shard_map/convert_element_type | solution.py:480
  68.0 6.5 %all-to-all-start = ((f16[8,784,128]{2,1,0:T(8,128)(2,1)}), f16[8,784,128]{2,1,0:T(8,128)(2,1)}, u32[]{:S(2)}, u32[]{:S(2)}) async-start(f16[8,784,128]{2,1,0:T(8,128)(2,1)} %convert_element_type.103), calls=%async_computation | async-start | bytes 3211264 | tf_op jit(solution)/shard_map/all_to_all | solution.py:479
  74.8 0.7 convert_element_type.105
  75.5 1.1 convert_element_type.106
  76.6 1.8 copy.109
  78.5 0.5 fusion.3.keep_ref
  78.9 5.2 %fusion.1.measured_ref = f32[2,384,1024]{2,1,0:T(8,128)} fusion(f32[2,384,1024]{2,1,0:T(8,128)S(1)} %bitcast.86, s32[1024]{0:T(1024)S(1)} %fusion.21), kind=kOutput, calls=%fused_computation.3 | convolution fusion | flops 4832886784 | bytes 6295552 | tf_op jit(solution)/shard_map/dot_general | solution.py:506
  84.2 28.7 %all-to-all-done = f16[8,784,128]{2,1,0:T(8,128)(2,1)} async-done(((f16[8,784,128]{2,1,0:T(8,128)(2,1)}), f16[8,784,128]{2,1,0:T(8,128)(2,1)}, u32[]{:S(2)}, u32[]{:S(2)}) %all-to-all-start) | async-done | bytes 1605664 | tf_op jit(solution)/shard_map/all_to_all | solution.py:479
  112.8 3.3 %convert_element_type.104.arrived_ref = f32[8,784,128]{2,1,0:T(8,128)} convert(f16[8,784,128]{2,1,0:T(8,128)(2,1)} %all-to-all-done) | non-fusion elementwise | flops 802816 | bytes 4816896 | tf_op jit(solution)/shard_map/convert_element_type | solution.py:482
  116.1 10.8 %rows.1 = f32[8,784,128]{2,1,0:T(8,128)} custom-call(f32[8,784,128]{2,1,0:T(8,128)} %convert_element_type.104.arrived_ref, f32[2,384,1024]{2,1,0:T(8,128)} %fusion.1.measured_ref, f32[96,1024]{1,0:T(8,128)S(1)} %fusion.3.keep_ref, bf16[1536,512]{1,0:T(8,128)(2,1)S(1)} %copy-done.2, bf16[1536,512]{1,0:T(8,128)(2,1)S(1)} %copy-done.1, f32[4,2,256]{2,1,0:T(2,128)S(1)} %copy-done.5), custom_call_target="tpu_custom_call" | custom-call | tf_op jit(solution)/shard_map/rows/pallas_call | solution.py:468
  127.0 2.1 %convert_element_type.110 = f16[8,784,128]{2,1,0:T(8,128)(2,1)S(1)} convert(f32[8,784,128]{2,1,0:T(8,128)} %rows.1) | non-fusion elementwise | flops 802816 | bytes 4816896 | tf_op jit(solution)/shard_map/convert_element_type | solution.py:480
  129.1 42.0 %all_to_all.10 = f16[8,784,128]{2,1,0:T(8,128)(2,1)S(1)} all-to-all(f16[8,784,128]{2,1,0:T(8,128)(2,1)S(1)} %convert_element_type.110), channel_id=1, replica_groups=mesh['grp'=2,'gz'=8,'col'=2] {'gz'}, dimensions={0} | all-to-all | bytes 3211264 | tf_op jit(solution)/shard_map/all_to_all | solution.py:479
  171.1 1.9 convert_element_type.111.arrived_ref
  173.2 7.1 %combine.1 = f32[2,128,768]{2,1,0:T(8,128)} custom-call(f32[8,784,128]{2,1,0:T(8,128)} %convert_element_type.111.arrived_ref, f32[4,2,128,768]{3,2,1,0:T(8,128)} %maps_ref.3, bf16[1536,512]{1,0:T(8,128)(2,1)S(1)} %copy-done, f32[3,2,256]{2,1,0:T(2,128)S(1)} %copy-done.4), custom_call_target="tpu_custom_call" | custom-call | tf_op jit(solution)/shard_map/combine/pallas_call | solution.py:468
  180.8 6.2 %reduce-scatter.2.cloned.1.call-done = f32[2,128,384]{2,1,0:T(8,128)} async-done(((f32[2,128,768]{2,1,0:T(8,128)}), f32[2,128,384]{2,1,0:T(8,128)}) %reduce-scatter.2.cloned.1.call-update) | async-done | bytes 393232 | tf_op jit(solution)/shard_map/reduce_scatter | solution.py:629
  187.0 1.8 multiply_add_fusion
  (119 shorter events, 6.9 us)
Async XLA Ops:
  7.6 9.6 %collective-permute-start = (bf16[2,3,384]{2,1,0:T(4,128)(2,1)S(1)}, bf16[2,3,384]{2,1,0:T(4,128)(2,1)S(1)}, u32[]{:S(2)}, u32[]{:S(2)}) collective-permute-start(bf16[2,3,384]{2,1,0:T(4,128)(2,1)S(1)} %get-tuple-element.28), channel_id=1, source_target_pairs={{0,2},{2,4},{4,6},{6,8},{8,10},{10,12},{12,14},{1,3},{3,5},{5,7},{... | collective-permute-start | bytes 13832 | tf_op jit(solution)/shard_map/ppermute | solution.py:30
  12.5 5.5 %collective-permute-start.1 = (bf16[2,3,384]{2,1,0:T(4,128)(2,1)S(1)}, bf16[2,3,384]{2,1,0:T(4,128)(2,1)S(1)}, u32[]{:S(2)}, u32[]{:S(2)}) collective-permute-start(bf16[2,3,384]{2,1,0:T(4,128)(2,1)S(1)} %get-tuple-element.29), channel_id=1, source_target_pairs={{2,0},{4,2},{6,4},{8,6},{10,8},{12,10},{14,12},{3,1},{5,3},{7,5},{... | collective-permute-start | bytes 13832 | tf_op jit(solution)/shard_map/ppermute | solution.py:33
  18.1 5.5 %collective-permute-start.2 = (bf16[2,134,3]{2,1,0:T(8,128)(2,1)S(1)}, bf16[2,134,3]{2,1,0:T(8,128)(2,1)S(1)}, u32[]{:S(2)}, u32[]{:S(2)}) collective-permute-start(bf16[2,134,3]{2,1,0:T(8,128)(2,1)S(1)} %get-tuple-element.26), channel_id=1, source_target_pairs={{0,1},{2,3},{4,5},{6,7},{8,9},{10,11},{12,13},{14,15},{16,17},{18,... | collective-permute-start | bytes 4832 | tf_op jit(solution)/shard_map/ppermute | solution.py:30
  19.4 4.2 %collective-permute-start.3 = (bf16[2,134,3]{2,1,0:T(8,128)(2,1)S(1)}, bf16[2,134,3]{2,1,0:T(8,128)(2,1)S(1)}, u32[]{:S(2)}, u32[]{:S(2)}) collective-permute-start(bf16[2,134,3]{2,1,0:T(8,128)(2,1)S(1)} %get-tuple-element.27), channel_id=1, source_target_pairs={{1,0},{3,2},{5,4},{7,6},{9,8},{11,10},{13,12},{15,14},{17,16},{19,... | collective-permute-start | bytes 4832 | tf_op jit(solution)/shard_map/ppermute | solution.py:33
  52.9 1.3 copy-start.9
  54.0 3.6 %copy-start.3 = (bf16[512,1536]{1,0:T(8,128)(2,1)S(1)}, bf16[512,1536]{1,0:T(8,128)(2,1)}, u32[]{:S(2)}) copy-start(bf16[512,1536]{1,0:T(8,128)(2,1)} %constant.95.clone.matrix_ref) | copy-start | bytes 4718596
  54.0 3.6 %copy-start.4 = (f32[3,2,256]{2,1,0:T(2,128)S(1)}, f32[3,2,256]{2,1,0:T(2,128)}, u32[]{:S(2)}) copy-start(f32[3,2,256]{2,1,0:T(2,128)} %constant.96.clone.twiddle_ref) | copy-start | bytes 18436
  54.3 10.3 %copy-start.6 = (f32[2,128,384]{2,1,0:T(8,128)}, f32[2,128,384]{2,1,0:T(8,128)S(1)}, u32[]{:S(2)}) copy-start(f32[2,128,384]{2,1,0:T(8,128)S(1)} %subtract_multiply_fusion) | copy-start | bytes 1179652
  64.6 10.1 %copy-start.11 = (s32[96,1024]{1,0:T(8,128)S(1)}, s32[96,1024]{1,0:T(8,128)}, u32[]{:S(2)}) copy-start(s32[96,1024]{1,0:T(8,128)} %param.18) | copy-start | bytes 1179652
  68.0 8.6 %copy-start.8 = (f32[2,96,4,1024]{3,2,1,0:T(4,128)S(1)}, f32[2,96,4,1024]{3,2,1,0:T(4,128)}, u32[]{:S(2)}) copy-start(f32[2,96,4,1024]{3,2,1,0:T(4,128)} %param.17) | copy-start | bytes 9437188
  68.0 44.8 %all-to-all-start = ((f16[8,784,128]{2,1,0:T(8,128)(2,1)}), f16[8,784,128]{2,1,0:T(8,128)(2,1)}, u32[]{:S(2)}, u32[]{:S(2)}) async-start(f16[8,784,128]{2,1,0:T(8,128)(2,1)} %convert_element_type.103), calls=%async_computation | async-start | bytes 3211264 | tf_op jit(solution)/shard_map/all_to_all | solution.py:479
  74.5 112.5 %reduce-scatter.2.cloned.1.call-start = ((), (), s32[]{:S(2)}) async-start(), calls=%async_computation.3 | async-start | bytes 1179648 | tf_op jit(solution)/shard_map/reduce_scatter | solution.py:629
  84.2 32.0 %copy-start.1 = (bf16[1536,512]{1,0:T(8,128)(2,1)S(1)}, bf16[1536,512]{1,0:T(8,128)(2,1)}, u32[]{:S(2)}) copy-start(bf16[1536,512]{1,0:T(8,128)(2,1)} %constant.98.clone.inverse_ref) | copy-start | bytes 4718596
  84.2 32.0 %copy-start.2 = (bf16[1536,512]{1,0:T(8,128)(2,1)S(1)}, bf16[1536,512]{1,0:T(8,128)(2,1)}, u32[]{:S(2)}) copy-start(bf16[1536,512]{1,0:T(8,128)(2,1)} %constant.97.clone.forward_ref) | copy-start | bytes 4718596
  84.2 32.0 %copy-start.5 = (f32[4,2,256]{2,1,0:T(2,128)S(1)}, f32[4,2,256]{2,1,0:T(2,128)}, u32[]{:S(2)}) copy-start(f32[4,2,256]{2,1,0:T(2,128)} %constant.99.clone.twiddle_ref) | copy-start | bytes 24580
  171.1 2.0 %copy-start = (bf16[1536,512]{1,0:T(8,128)(2,1)S(1)}, bf16[1536,512]{1,0:T(8,128)(2,1)}, u32[]{:S(2)}) copy-start(bf16[1536,512]{1,0:T(8,128)(2,1)} %constant.100.clone.matrix_ref) | copy-start | bytes 4718596
  173.1 7.1 %copy-start.10 = (f32[32,8,384]{2,1,0:T(8,128)S(1)}, f32[32,8,384]{2,1,0:T(8,128)}, u32[]{:S(2)}) copy-start(f32[32,8,384]{2,1,0:T(8,128)} %get-tuple-element.21) | copy-start | bytes 1179652
  180.3 6.7 %copy-start.7 = (f32[2,128,384]{2,1,0:T(8,128)S(1)}, f32[2,128,384]{2,1,0:T(8,128)}, u32[]{:S(2)}) copy-start(f32[2,128,384]{2,1,0:T(8,128)} %copy-done.6) | copy-start | bytes 1179652
  180.3 6.7 %copy-start.12 = (f32[2,128,384]{2,1,0:T(8,128)S(1)}, f32[2,128,384]{2,1,0:T(8,128)}, u32[]{:S(2)}) copy-start(f32[2,128,384]{2,1,0:T(8,128)} %param.15) | copy-start | bytes 1179652
Sparse Core Ops, SparseCore 0:
  180.4 6.5 reduce-scatter.1
where the time goes:
time: 196 us
  Pallas kernels  50.7 us (26%)
  blocking collectives  45.3 us (23%)
  waiting for transfers between devices  35.6 us (18%)
  other arithmetic  17.9 us (9%)
  starting transfers between devices  15.5 us (8%)
  between operations  14.1 us (7%)
  local copies, waits for them, and re-layouts  10.9 us (6%)
  matrix products  5.68 us (3%)
    all_to_all x1, blocking collectives, exchange(): lax.all_to_all(values.astype(jnp.float16), 'gz', split_axis=0, concat_axi...  42 us
    all_to_all x1, waiting for transfers between devices, exchange(): lax.all_to_all(values.astype(jnp.float16), 'gz', split_axis=0, concat_axi...  28.7 us
    pallas_call x1, Pallas kernels, network(): pl.pallas_call(partial(network_kernel, groups, cols), out_shape=jax.Shape...  25.7 us
    pallas_call x3, Pallas kernels, call_whole(): pl.pallas_call(kernel, out_shape=jax.ShapeDtypeStruct(shape, jnp.float32)...  25 us
    all_to_all x1, starting transfers between devices, exchange(): lax.all_to_all(values.astype(jnp.float16), 'gz', split_axis=0, concat_axi...  6.51 us
    reduce_scatter x1, waiting for transfers between devices, local(): grad_tile = lax.psum_scatter(grad, 'col', scatter_dimension=2, tiled=True)  6.19 us
    ppermute x2, starting transfers between devices, with_halo(): lax.ppermute(lax.slice_in_dim(block, block.shape[dim] - width, None, axis...  6.16 us
    convert_element_type x2, other arithmetic, exchange(): values.astype(jnp.float16)  5.52 us
  transfers between devices with their start and end apart: 6, of which 3 were waited for; matrix products, arithmetic and copies ran while one was open for 8% of the time, Pallas kernels for 0%

commit v1 on v0

--- a/solution.py
+++ b/solution.py
@@ -412,7 +412,8 @@
     level_out(out_ref, 2 * vectors)
 
 
-def combine_kernel(arrived_ref, maps_ref, matrix_ref, twiddle_ref, out_ref):
+def combine_kernel(arrived_ref, maps_ref, matrix_ref, twiddle_ref, *refs):
+    earlier_ref, out_ref = refs if len(refs) == 2 else (None, refs[0])
     coils, _, rows, full = maps_ref.shape
     groups = arrived_ref.shape[0]
     inner = full // 3
@@ -449,28 +450,49 @@
         (middle[0] - apart[1], middle[1] + apart[0]),
         (middle[0] + apart[1], middle[1] - apart[0]),
     )
-    for n in range(3):
-        lanes = slice(n * inner, (n + 1) * inner)
-        real = imag = None
+    share = out_ref.shape[3]
+    for start in range(0, full, 128):
+        n, inside = start // inner, slice(start % inner, start % inner + 128)
+        lanes = slice(start, start + 128)
+        half, place = start // share, slice(start % share, start % share + 128)
+        real = 0.0 if earlier_ref is None else earlier_ref[half, 0, :, place]
+        imag = 0.0 if earlier_ref is None else earlier_ref[half, 1, :, place]
         for coil in range(coils):
-            back = [blocks[n][part][coil * rows : (coil + 1) * rows] for part in range(2)]
+            back = [
+                blocks[n][part][coil * rows : (coil + 1) * rows, inside] for part in range(2)
+            ]
             map_real = maps_ref[coil, 0, :, lanes]
             map_imag = maps_ref[coil, 1, :, lanes]
-            term_real = map_real * back[0] + map_imag * back[1]
-            term_imag = map_real * back[1] - map_imag * back[0]
-            real = term_real if real is None else real + term_real
-            imag = term_imag if imag is None else imag + term_imag
-        out_ref[0, :, lanes] = real
-        out_ref[1, :, lanes] = imag
-
-
-def call_whole(kernel, shape, name, *operands):
+            real = real + map_real * back[0] + map_imag * back[1]
+            imag = imag + map_real * back[1] - map_imag * back[0]
+        out_ref[half, 0, :, place] = real
+        out_ref[half, 1, :, place] = imag
+
+
+def whole_block(operand):
+    return pl.BlockSpec(operand.shape, lambda i: (0,) * operand.ndim)
+
+
+def part_block(operand, axis, parts, index):
+    block = list(operand.shape)
+    block[axis] //= parts
+    return pl.BlockSpec(
+        tuple(block), lambda i: tuple(index if a == axis else 0 for a in range(operand.ndim))
+    )
+
+
+def call_whole(kernel, shape, name, flops, *operands, specs=None):
+    specs = specs or {}
     return pl.pallas_call(
         kernel,
+        grid=(1,),
         out_shape=jax.ShapeDtypeStruct(shape, jnp.float32),
-        in_specs=[pl.BlockSpec(memory_space=pltpu.VMEM)] * len(operands),
-        out_specs=pl.BlockSpec(memory_space=pltpu.VMEM),
+        in_specs=[specs.get(i) or whole_block(operand) for i, operand in enumerate(operands)],
+        out_specs=pl.BlockSpec(shape, lambda i: (0,) * len(shape)),
         compiler_params=pltpu.CompilerParams(vmem_limit_bytes=50 * 1024 * 1024),
+        cost_estimate=pl.CostEstimate(
+            flops=flops, bytes_accessed=8 * math.prod(shape), transcendentals=0
+        ),
         name=name,
     )(*operands)
 
@@ -488,56 +510,72 @@
     height = rows * groups
     inner = full // 3
     piece = inner // groups
-    vectors = coils * 3 * piece
+    parts = 2
+    vectors = coils // parts * 3 * piece
     sent = (groups, 2 * vectors + 16, rows)
+    flops = 12 * vectors * inner * rows * groups
     high, low = pair_matrix(inner, full, False)
     left = np.concatenate([high, high, low], axis=1)
     right = np.concatenate([high, high, low], axis=0)
     columns_twiddles = twiddle_rows(3, inner)
-    spectra = call_whole(
-        columns_kernel, sent, "columns", clean_wide, coil_maps, left, columns_twiddles
-    )
-    measured, sampled, spectra = lax.optimization_barrier((measured, sampled, spectra))
-    arrived = exchange(spectra)
+    rows_high, rows_low = pair_matrix(height // 4, height, True)
+    back_high, back_low = pair_matrix(height // 4, height, False)
+    forward = np.concatenate([rows_high, rows_high, rows_low], axis=0)
+    inverse = np.concatenate([back_high, back_high, back_low], axis=0)
+    rows_twiddles = twiddle_rows(4, height // 4)
+    spectra = []
+    for part in range(parts):
+        maps = {1: part_block(coil_maps, 0, parts, part)}
+        operands = (clean_wide, coil_maps, left, columns_twiddles)
+        spectra.append(
+            call_whole(columns_kernel, sent, "columns", flops, *operands, specs=maps)
+        )
+        if part == 0:
+            measured, sampled, spectra[0] = lax.optimization_barrier(
+                (measured, sampled, spectra[0])
+            )
+    arrived = [exchange(values) for values in spectra]
+    arrived[0], spectra[1] = lax.optimization_barrier((arrived[0], spectra[1]))
     place = jnp.arange(height)
     source = place // (height // 4) + 4 * (place % (height // 4))
     permute = (place[:, None] == source[None, :]).astype(jnp.float32)
     targets = jnp.transpose(measured.reshape(2, piece, 3, coils, height), (0, 3, 2, 1, 4))
     targets = jnp.dot(
-        targets.reshape(2 * vectors, height), permute, precision=lax.Precision.HIGH
-    ).reshape(2, vectors, height)
+        targets.reshape(2 * parts * vectors, height), permute, precision=lax.Precision.HIGH
+    ).reshape(2, parts * vectors, height)
     keep = jnp.transpose(sampled.reshape(piece, 3, height), (1, 0, 2)).astype(jnp.bfloat16)
     keep = jnp.dot(
         keep.reshape(3 * piece, height),
         permute.astype(jnp.bfloat16),
         preferred_element_type=jnp.float32,
     )
-    rows_high, rows_low = pair_matrix(height // 4, height, True)
-    back_high, back_low = pair_matrix(height // 4, height, False)
-    residual = call_whole(
-        rows_kernel,
-        sent,
-        "rows",
-        arrived,
-        targets,
-        keep,
-        np.concatenate([rows_high, rows_high, rows_low], axis=0),
-        np.concatenate([back_high, back_high, back_low], axis=0),
-        twiddle_rows(4, height // 4),
-    )
-    arrived = exchange(residual)
-    return call_whole(
-        combine_kernel, (2, rows, full), "combine", arrived, coil_maps, right, columns_twiddles
-    )
+    residual = []
+    for part in range(parts):
+        target = {1: part_block(targets, 1, parts, part)}
+        operands = (arrived[part], targets, keep, forward, inverse, rows_twiddles)
+        residual.append(
+            call_whole(rows_kernel, sent, "rows", 2 * flops, *operands, specs=target)
+        )
+    arrived = [exchange(values) for values in residual]
+    arrived[0], residual[1] = lax.optimization_barrier((arrived[0], residual[1]))
+    halves = lax.axis_size("col")
+    total = ()
+    for part in range(parts):
+        maps = {1: part_block(coil_maps, 0, parts, part)}
+        operands = (arrived[part], coil_maps, right, columns_twiddles) + total
+        shape = (halves, 2, rows, full // halves)
+        total = (call_whole(combine_kernel, shape, "combine", flops, *operands, specs=maps),)
+    return total[0]
 
 
 def gradient(clean_wide, coil_maps, measured, sampled):
     coils, _, rows, full = coil_maps.shape
     groups = lax.axis_size("gz")
-    whole = rows % 128 == 0 and coils % 2 == 0 and full % 768 == 0
+    whole = rows % 128 == 0 and coils % 4 == 0 and full % 768 == 0
     if whole and (rows * groups) % 1024 == 0 and full % (48 * groups) == 0:
         return aligned_gradient(clean_wide, coil_maps, measured, sampled)
-    return plain_gradient(clean_wide, coil_maps, measured, sampled)
+    grad = plain_gradient(clean_wide, coil_maps, measured, sampled)
+    return jnp.stack(jnp.split(grad, lax.axis_size("col"), axis=2))
 
 
 def plain_gradient(clean_wide, coil_maps, measured, sampled):
@@ -626,9 +664,13 @@
     clean = (noisy_image - SIGMA_NOW * predicted) / SCALE_NOW
     clean_wide = lax.all_gather(clean, "col", axis=2, tiled=True)
     grad = gradient(clean_wide, coil_maps, measured, sampled)
-    grad_tile = lax.psum_scatter(
-        grad, "col", scatter_dimension=2, tiled=True
-    )
+    if lax.axis_size("col") == 2:
+        here = lax.axis_index("col")
+        away = lax.dynamic_index_in_dim(grad, 1 - here, 0, keepdims=False)
+        grad_tile = lax.dynamic_index_in_dim(grad, here, 0, keepdims=False)
+        grad_tile = grad_tile + lax.ppermute(away, "col", [(0, 1), (1, 0)])
+    else:
+        grad_tile = lax.psum_scatter(grad, "col", scatter_dimension=0, tiled=False)
     update = clean - STEP_GAIN * grad_tile
     return SCALE_NEXT * update + DIRECT_GAIN * predicted + NOISE_GAIN * fresh_noise
 

time: 196 us -> 173 us (0.88)
  blocking collectives: 45.3 us -> 3.11 us
  starting transfers between devices: 15.5 us -> 28.9 us
  between operations: 14.1 us -> 0.8 us
  waiting for transfers between devices: 35.6 us -> 44 us
  local copies, waits for them, and re-layouts: 10.9 us -> 14.5 us
  other arithmetic: 17.9 us -> 20.2 us
    all_to_all x1 -> x0, blocking collectives: 42 us -> none  [exchange(): lax.all_to_all(values.astype(jnp.float16), 'gz', split_axis=0, concat_axi...]
    all_to_all x1 -> x4, starting transfers between devices: 6.51 us -> 20.1 us  [exchange(): lax.all_to_all(values.astype(jnp.float16), 'gz', split_axis=0, concat_axi...]
    all_to_all x1 -> x4, waiting for transfers between devices: 28.7 us -> 41.4 us  [exchange(): lax.all_to_all(values.astype(jnp.float16), 'gz', split_axis=0, concat_axi...]
    reduce_scatter x1 -> x0, waiting for transfers between devices: 6.19 us -> none  [local(): grad_tile = lax.psum_scatter(grad, 'col', scatter_dimension=2, tiled=True)]
    transpose x1, local copies, waits for them, and re-layouts: 1.82 us -> 5.46 us  [aligned_gradient(): jnp.transpose(measured.reshape(2, piece, 3, coils, height), (0, 3, 2, 1, 4))]
    convert_element_type x2 -> x4, other arithmetic: 5.14 us -> 7.58 us  [exchange(): return moved.astype(jnp.float32)]
    pallas_call x3 -> x6, Pallas kernels: 25 us -> 26.9 us  [call_whole(): pl.pallas_call(kernel, grid=(1,), out_shape=jax.ShapeDtypeStruct(shape, j...]
    convert_element_type x2 -> x4, other arithmetic: 5.52 us -> 7.02 us  [exchange(): values.astype(jnp.float16)]
  transfers between devices with their start and end apart: 6 -> 9, of which waited for: 3 -> 5; matrix products, arithmetic and copies ran while one was open for 8% -> 18% of each run, Pallas kernels for 0% -> 12%
where the time goes in v1:
time: 173 us; the launch traced here: 172 us
  Pallas kernels  52.6 us (30%)
  waiting for transfers between devices  44 us (25%)
  starting transfers between devices  28.9 us (17%)
  other arithmetic  20.2 us (12%)
  local copies, waits for them, and re-layouts  14.5 us (8%)
  matrix products  7.63 us (4%)
  blocking collectives  3.11 us (2%)
    all_to_all x4, waiting for transfers between devices, exchange(): lax.all_to_all(values.astype(jnp.float16), 'gz', split_axis=0, concat_axi...  41.4 us
    pallas_call x6, Pallas kernels, call_whole(): pl.pallas_call(kernel, grid=(1,), out_shape=jax.ShapeDtypeStruct(shape, j...  26.9 us
    pallas_call x1, Pallas kernels, network(): pl.pallas_call(partial(network_kernel, groups, cols), out_shape=jax.Shape...  25.7 us
    all_to_all x4, starting transfers between devices, exchange(): lax.all_to_all(values.astype(jnp.float16), 'gz', split_axis=0, concat_axi...  20.1 us
    convert_element_type x4, other arithmetic, exchange(): return moved.astype(jnp.float32)  7.58 us
    dot_general x1, matrix products, aligned_gradient(): jnp.dot(targets.reshape(2 * parts * vectors, height), permute, precision=...  7.16 us
    convert_element_type x4, other arithmetic, exchange(): values.astype(jnp.float16)  7.02 us
    ppermute x2, starting transfers between devices, with_halo(): lax.ppermute(lax.slice_in_dim(block, block.shape[dim] - width, None, axis...  6.16 us
  transfers between devices with their start and end apart: 9, of which 5 were waited for; matrix products, arithmetic and copies ran while one was open for 18% of the time, Pallas kernels for 12%

profile of v1, /device:TPU:0, one launch (start us, length us, event | category | flops | bytes accessed | tf_op | source)
XLA Modules:
  0.0 171.8 jit_solution(3014202174265102454)
XLA Ops:
  0.0 1.0 convert_element_type.111
  1.1 4.9 %collective-permute-start = (bf16[2,3,384]{2,1,0:T(4,128)(2,1)S(1)}, bf16[2,3,384]{2,1,0:T(4,128)(2,1)S(1)}, u32[]{:S(2)}, u32[]{:S(2)}) collective-permute-start(bf16[2,3,384]{2,1,0:T(4,128)(2,1)S(1)} %get-tuple-element.32), channel_id=1, source_target_pairs={{0,2},{2,4},{4,6},{6,8},{8,10},{10,12},{12,14},{1,3},{3,5},{5,7},{... | collective-permute-start | bytes 13832 | tf_op jit(solution)/shard_map/ppermute | solution.py:30
  5.9 1.3 collective-permute-start.1
  10.0 1.4 collective-permute-done.1
  11.6 1.3 collective-permute-start.2
  12.9 1.3 collective-permute-start.3
  20.7 25.7 %network.1 = f32[32,8,384]{2,1,0:T(8,128)S(1)} custom-call(bf16[9,400,128]{2,1,0:T(8,128)(2,1)S(1)} %pad.113.tiles_ref, bf16[4,128,256]{2,1,0:T(8,128)(2,1)S(1)} %pad.130.first_ref, bf16[3,384,256]{2,1,0:T(8,128)(2,1)S(1)} %reshape.111.inner_ref, bf16[32,384]{1,0:T(8,128)(2,1)S(1)} %pad.139.last_ref, f32[36,1,256]{2,1,0:T(1,128)S(1)} %reshape_reshape.6.first_rows_ref, ...), custom_call_target="tpu_custom_call" | custom-call | tf_op jit(solution)/shard_map/network/pallas_call | solution.py:168
  48.6 3.1 %all_gather.3.clean_ref = f32[2,128,768]{2,1,0:T(8,128)S(1)} all-gather(f32[2,128,384]{2,1,0:T(8,128)S(1)} %subtract_multiply_fusion), channel_id=1, replica_groups=mesh['grp'=2,'gz'=8,'col'=2] {'col'}, dimensions={2}, use_global_device_ids=true | all-gather | bytes 1179648 | tf_op jit(solution)/shard_map/all_gather | solution.py:665
  51.7 3.4 %columns.3 = f32[8,400,128]{2,1,0:T(8,128)S(1)} custom-call(f32[2,128,768]{2,1,0:T(8,128)S(1)} %all_gather.3.clean_ref, f32[4,2,128,768]{3,2,1,0:T(8,128)} %maps_ref.7, bf16[512,1536]{1,0:T(8,128)(2,1)S(1)} %copy-done, f32[3,2,256]{2,1,0:T(2,128)S(1)} %copy-done.4), custom_call_target="tpu_custom_call" | custom-call | flops 603979776 | bytes 3276800 | tf_op jit(solution)/shard_map/columns/pallas_call | solution.py:486
  55.0 1.0 convert_element_type.124
  56.0 5.7 %all-to-all-start.2 = ((f16[8,400,128]{2,1,0:T(8,128)(2,1)}), f16[8,400,128]{2,1,0:T(8,128)(2,1)S(1)}, u32[]{:S(2)}, u32[]{:S(2)}) async-start(f16[8,400,128]{2,1,0:T(8,128)(2,1)} %convert_element_type.124), calls=%async_computation.2 | async-start | bytes 1638400 | tf_op jit(solution)/shard_map/all_to_all | solution.py:501
  61.8 3.4 %columns.2 = f32[8,400,128]{2,1,0:T(8,128)S(1)} custom-call(f32[2,128,768]{2,1,0:T(8,128)S(1)} %all_gather.3.clean_ref, f32[4,2,128,768]{3,2,1,0:T(8,128)} %maps_ref.7, bf16[512,1536]{1,0:T(8,128)(2,1)S(1)} %copy-done, f32[3,2,256]{2,1,0:T(2,128)S(1)} %copy-done.4), custom_call_target="tpu_custom_call" | custom-call | flops 603979776 | bytes 3276800 | tf_op jit(solution)/shard_map/columns/pallas_call | solution.py:486
  65.1 1.1 convert_element_type.115
  66.2 16.9 %all-to-all-done.2 = f16[8,400,128]{2,1,0:T(8,128)(2,1)S(1)} async-done(((f16[8,400,128]{2,1,0:T(8,128)(2,1)}), f16[8,400,128]{2,1,0:T(8,128)(2,1)S(1)}, u32[]{:S(2)}, u32[]{:S(2)}) %all-to-all-start.2) | async-done | bytes 819232 | tf_op jit(solution)/shard_map/all_to_all | solution.py:501
  83.2 4.2 %all-to-all-start = ((f16[8,400,128]{2,1,0:T(8,128)(2,1)}), f16[8,400,128]{2,1,0:T(8,128)(2,1)}, u32[]{:S(2)}, u32[]{:S(2)}) async-start(f16[8,400,128]{2,1,0:T(8,128)(2,1)} %convert_element_type.115), calls=%async_computation | async-start | bytes 1638400 | tf_op jit(solution)/shard_map/all_to_all | solution.py:501
  87.4 5.5 %copy.109 = f32[2,4,3,32,1024]{4,3,2,1,0:T(8,128)} copy(f32[2,4,3,32,1024]{4,1,2,3,0:T(4,128)} %bitcast.97) | data formatting | bytes 6291456 | tf_op jit(solution)/shard_map/transpose | solution.py:542
  93.6 7.2 %fusion.1.measured_ref = f32[2,384,1024]{2,1,0:T(8,128)} fusion(f32[2,384,1024]{2,1,0:T(8,128)} %bitcast.98, s32[1024]{0:T(1024)S(1)} %fusion.25), kind=kOutput, calls=%fused_computation.3 | convolution fusion | flops 4832886784 | bytes 6295552 | tf_op jit(solution)/shard_map/dot_general | solution.py:543
  100.8 1.3 convert_element_type.125.arrived_ref
  102.8 6.6 %rows.3 = f32[8,400,128]{2,1,0:T(8,128)} custom-call(f32[8,400,128]{2,1,0:T(8,128)} %convert_element_type.125.arrived_ref, f32[2,384,1024]{2,1,0:T(8,128)} %fusion.1.measured_ref, f32[96,1024]{1,0:T(8,128)S(1)} %fusion.3.keep_ref, bf16[1536,512]{1,0:T(8,128)(2,1)S(1)} %copy-done.2, bf16[1536,512]{1,0:T(8,128)(2,1)S(1)} %copy-done.3, f32[4,2,256]{2,1,0:T(2,128)S(1)} %copy-done.5), custom_call_target="tpu_custom_call" | custom-call | flops 1207959552 | bytes 3276800 | tf_op jit(solution)/shard_map/rows/pallas_call | solution.py:486
  109.4 2.5 %convert_element_type.126 = f16[8,400,128]{2,1,0:T(8,128)(2,1)} convert(f32[8,400,128]{2,1,0:T(8,128)} %rows.3) | non-fusion elementwise | flops 409600 | bytes 2457600 | tf_op jit(solution)/shard_map/convert_element_type | solution.py:502
  112.0 5.9 %all-to-all-start.3 = ((f16[8,400,128]{2,1,0:T(8,128)(2,1)}), f16[8,400,128]{2,1,0:T(8,128)(2,1)}, u32[]{:S(2)}, u32[]{:S(2)}) async-start(f16[8,400,128]{2,1,0:T(8,128)(2,1)} %convert_element_type.126), calls=%async_computation.3 | async-start | bytes 1638400 | tf_op jit(solution)/shard_map/all_to_all | solution.py:501
  117.9 2.4 %convert_element_type.116.arrived_ref = f32[8,400,128]{2,1,0:T(8,128)} convert(f16[8,400,128]{2,1,0:T(8,128)(2,1)} %all-to-all-done) | non-fusion elementwise | flops 409600 | bytes 2457600 | tf_op jit(solution)/shard_map/convert_element_type | solution.py:504
  120.3 6.7 %rows.2 = f32[8,400,128]{2,1,0:T(8,128)} custom-call(f32[8,400,128]{2,1,0:T(8,128)} %convert_element_type.116.arrived_ref, f32[2,384,1024]{2,1,0:T(8,128)} %fusion.1.measured_ref, f32[96,1024]{1,0:T(8,128)S(1)} %fusion.3.keep_ref, bf16[1536,512]{1,0:T(8,128)(2,1)S(1)} %copy-done.2, bf16[1536,512]{1,0:T(8,128)(2,1)S(1)} %copy-done.3, f32[4,2,256]{2,1,0:T(2,128)S(1)} %copy-done.5), custom_call_target="tpu_custom_call" | custom-call | flops 1207959552 | bytes 3276800 | tf_op jit(solution)/shard_map/rows/pallas_call | solution.py:486
  127.0 2.4 %convert_element_type.122 = f16[8,400,128]{2,1,0:T(8,128)(2,1)} convert(f32[8,400,128]{2,1,0:T(8,128)} %rows.2) | non-fusion elementwise | flops 409600 | bytes 2457600 | tf_op jit(solution)/shard_map/convert_element_type | solution.py:502
  129.4 8.7 %all-to-all-done.3 = f16[8,400,128]{2,1,0:T(8,128)(2,1)} async-done(((f16[8,400,128]{2,1,0:T(8,128)(2,1)}), f16[8,400,128]{2,1,0:T(8,128)(2,1)}, u32[]{:S(2)}, u32[]{:S(2)}) %all-to-all-start.3) | async-done | bytes 819232 | tf_op jit(solution)/shard_map/all_to_all | solution.py:501
  138.1 4.2 %all-to-all-start.1 = ((f16[8,400,128]{2,1,0:T(8,128)(2,1)}), f16[8,400,128]{2,1,0:T(8,128)(2,1)}, u32[]{:S(2)}, u32[]{:S(2)}) async-start(f16[8,400,128]{2,1,0:T(8,128)(2,1)} %convert_element_type.122), calls=%async_computation.1 | async-start | bytes 1638400 | tf_op jit(solution)/shard_map/all_to_all | solution.py:501
  142.3 1.4 convert_element_type.127.arrived_ref
  144.0 3.2 %combine.2.refs_0_ = f32[2,2,128,384]{3,2,1,0:T(8,128)S(1)} custom-call(f32[8,400,128]{2,1,0:T(8,128)S(1)} %convert_element_type.127.arrived_ref, f32[4,2,128,768]{3,2,1,0:T(8,128)} %maps_ref.7, bf16[1536,512]{1,0:T(8,128)(2,1)S(1)} %copy-done.1, f32[3,2,256]{2,1,0:T(2,128)S(1)} %copy-done.4), custom_call_target="tpu_custom_call" | custom-call | flops 603979776 | bytes 1572864 | tf_op jit(solution)/shard_map/combine/pallas_call | solution.py:486
  147.1 15.7 %all-to-all-done.1 = f16[8,400,128]{2,1,0:T(8,128)(2,1)} async-done(((f16[8,400,128]{2,1,0:T(8,128)(2,1)}), f16[8,400,128]{2,1,0:T(8,128)(2,1)}, u32[]{:S(2)}, u32[]{:S(2)}) %all-to-all-start.1) | async-done | bytes 819232 | tf_op jit(solution)/shard_map/all_to_all | solution.py:501
  162.9 2.5 %convert_element_type.123.arrived_ref = f32[8,400,128]{2,1,0:T(8,128)} convert(f16[8,400,128]{2,1,0:T(8,128)(2,1)} %all-to-all-done.1) | non-fusion elementwise | flops 409600 | bytes 2457600 | tf_op jit(solution)/shard_map/convert_element_type | solution.py:504
  165.3 3.7 %combine.3 = f32[2,2,128,384]{3,2,1,0:T(8,128)S(1)} custom-call(f32[8,400,128]{2,1,0:T(8,128)} %convert_element_type.123.arrived_ref, f32[4,2,128,768]{3,2,1,0:T(8,128)} %maps_ref.7, bf16[1536,512]{1,0:T(8,128)(2,1)S(1)} %copy-done.1, f32[3,2,256]{2,1,0:T(2,128)S(1)} %copy-done.4, f32[2,2,128,384]{3,2,1,0:T(8,128)S(1)} %combine.2.refs_0_), custom_call_target="tpu_custom_call" | custom-call | flops 603979776 | bytes 1572864 | tf_op jit(solution)/shard_map/combine/pallas_call | solution.py:486
  169.7 1.2 collective-permute-done.4
  (135 shorter events, 14.1 us)
Async XLA Ops:
  0.0 9.5 %copy-start.14 = (bf16[9,2,64]{2,1,0:T(2,128)(2,1)S(1)}, bf16[9,2,64]{2,1,0:T(2,128)(2,1)}, u32[]{:S(2)}) copy-start(bf16[9,2,64]{2,1,0:T(2,128)(2,1)} %param.21) | copy-start | bytes 6916
  1.1 9.0 %collective-permute-start = (bf16[2,3,384]{2,1,0:T(4,128)(2,1)S(1)}, bf16[2,3,384]{2,1,0:T(4,128)(2,1)S(1)}, u32[]{:S(2)}, u32[]{:S(2)}) collective-permute-start(bf16[2,3,384]{2,1,0:T(4,128)(2,1)S(1)} %get-tuple-element.32), channel_id=1, source_target_pairs={{0,2},{2,4},{4,6},{6,8},{8,10},{10,12},{12,14},{1,3},{3,5},{5,7},{... | collective-permute-start | bytes 13832 | tf_op jit(solution)/shard_map/ppermute | solution.py:30
  5.9 5.5 %collective-permute-start.1 = (bf16[2,3,384]{2,1,0:T(4,128)(2,1)S(1)}, bf16[2,3,384]{2,1,0:T(4,128)(2,1)S(1)}, u32[]{:S(2)}, u32[]{:S(2)}) collective-permute-start(bf16[2,3,384]{2,1,0:T(4,128)(2,1)S(1)} %get-tuple-element.33), channel_id=1, source_target_pairs={{2,0},{4,2},{6,4},{8,6},{10,8},{12,10},{14,12},{3,1},{5,3},{7,5},{... | collective-permute-start | bytes 13832 | tf_op jit(solution)/shard_map/ppermute | solution.py:33
  11.6 5.5 %collective-permute-start.2 = (bf16[2,134,3]{2,1,0:T(8,128)(2,1)S(1)}, bf16[2,134,3]{2,1,0:T(8,128)(2,1)S(1)}, u32[]{:S(2)}, u32[]{:S(2)}) collective-permute-start(bf16[2,134,3]{2,1,0:T(8,128)(2,1)S(1)} %get-tuple-element.30), channel_id=1, source_target_pairs={{0,1},{2,3},{4,5},{6,7},{8,9},{10,11},{12,13},{14,15},{16,17},{18,... | collective-permute-start | bytes 4832 | tf_op jit(solution)/shard_map/ppermute | solution.py:30
  12.9 4.2 %collective-permute-start.3 = (bf16[2,134,3]{2,1,0:T(8,128)(2,1)S(1)}, bf16[2,134,3]{2,1,0:T(8,128)(2,1)S(1)}, u32[]{:S(2)}, u32[]{:S(2)}) collective-permute-start(bf16[2,134,3]{2,1,0:T(8,128)(2,1)S(1)} %get-tuple-element.31), channel_id=1, source_target_pairs={{1,0},{3,2},{5,4},{7,6},{9,8},{11,10},{13,12},{15,14},{17,16},{19,... | collective-permute-start | bytes 4832 | tf_op jit(solution)/shard_map/ppermute | solution.py:33
  46.4 1.3 copy-start.10
  47.6 4.1 %copy-start = (bf16[512,1536]{1,0:T(8,128)(2,1)S(1)}, bf16[512,1536]{1,0:T(8,128)(2,1)}, u32[]{:S(2)}) copy-start(bf16[512,1536]{1,0:T(8,128)(2,1)} %constant.105.clone.matrix_ref) | copy-start | bytes 4718596
  47.6 4.1 %copy-start.4 = (f32[3,2,256]{2,1,0:T(2,128)S(1)}, f32[3,2,256]{2,1,0:T(2,128)}, u32[]{:S(2)}) copy-start(f32[3,2,256]{2,1,0:T(2,128)} %constant.106.clone.twiddle_ref) | copy-start | bytes 18436
  47.8 0.7 copy-start.6
  56.0 27.1 %all-to-all-start.2 = ((f16[8,400,128]{2,1,0:T(8,128)(2,1)}), f16[8,400,128]{2,1,0:T(8,128)(2,1)S(1)}, u32[]{:S(2)}, u32[]{:S(2)}) async-start(f16[8,400,128]{2,1,0:T(8,128)(2,1)} %convert_element_type.124), calls=%async_computation.2 | async-start | bytes 1638400 | tf_op jit(solution)/shard_map/all_to_all | solution.py:501
  83.2 9.7 %copy-start.8 = (f16[8,400,128]{2,1,0:T(8,128)(2,1)}, f16[8,400,128]{2,1,0:T(8,128)(2,1)S(1)}, u32[]{:S(2)}) copy-start(f16[8,400,128]{2,1,0:T(8,128)(2,1)S(1)} %all-to-all-done.2) | copy-start | bytes 2457604
  83.2 28.8 %all-to-all-start = ((f16[8,400,128]{2,1,0:T(8,128)(2,1)}), f16[8,400,128]{2,1,0:T(8,128)(2,1)}, u32[]{:S(2)}, u32[]{:S(2)}) async-start(f16[8,400,128]{2,1,0:T(8,128)(2,1)} %convert_element_type.115), calls=%async_computation | async-start | bytes 1638400 | tf_op jit(solution)/shard_map/all_to_all | solution.py:501
  87.4 5.5 %copy-start.13 = (s32[96,1024]{1,0:T(8,128)S(1)}, s32[96,1024]{1,0:T(8,128)}, u32[]{:S(2)}) copy-start(s32[96,1024]{1,0:T(8,128)} %param.18) | copy-start | bytes 1179652
  93.6 7.2 %copy-start.9 = (f16[8,400,128]{2,1,0:T(8,128)(2,1)S(1)}, f16[8,400,128]{2,1,0:T(8,128)(2,1)}, u32[]{:S(2)}) copy-start(f16[8,400,128]{2,1,0:T(8,128)(2,1)} %copy-done.8) | copy-start | bytes 2457604
  93.6 8.5 %copy-start.3 = (bf16[1536,512]{1,0:T(8,128)(2,1)S(1)}, bf16[1536,512]{1,0:T(8,128)(2,1)}, u32[]{:S(2)}) copy-start(bf16[1536,512]{1,0:T(8,128)(2,1)} %constant.108.clone.inverse_ref) | copy-start | bytes 4718596
  100.8 2.0 %copy-start.2 = (bf16[1536,512]{1,0:T(8,128)(2,1)S(1)}, bf16[1536,512]{1,0:T(8,128)(2,1)}, u32[]{:S(2)}) copy-start(bf16[1536,512]{1,0:T(8,128)(2,1)} %constant.107.clone.forward_ref) | copy-start | bytes 4718596
  100.8 2.0 %copy-start.5 = (f32[4,2,256]{2,1,0:T(2,128)S(1)}, f32[4,2,256]{2,1,0:T(2,128)}, u32[]{:S(2)}) copy-start(f32[4,2,256]{2,1,0:T(2,128)} %constant.109.clone.twiddle_ref) | copy-start | bytes 24580
  112.0 26.1 %all-to-all-start.3 = ((f16[8,400,128]{2,1,0:T(8,128)(2,1)}), f16[8,400,128]{2,1,0:T(8,128)(2,1)}, u32[]{:S(2)}, u32[]{:S(2)}) async-start(f16[8,400,128]{2,1,0:T(8,128)(2,1)} %convert_element_type.126), calls=%async_computation.3 | async-start | bytes 1638400 | tf_op jit(solution)/shard_map/all_to_all | solution.py:501
  138.1 24.8 %all-to-all-start.1 = ((f16[8,400,128]{2,1,0:T(8,128)(2,1)}), f16[8,400,128]{2,1,0:T(8,128)(2,1)}, u32[]{:S(2)}, u32[]{:S(2)}) async-start(f16[8,400,128]{2,1,0:T(8,128)(2,1)} %convert_element_type.122), calls=%async_computation.1 | async-start | bytes 1638400 | tf_op jit(solution)/shard_map/all_to_all | solution.py:501
  142.3 1.7 copy-start.1
  165.3 3.9 %copy-start.11 = (f32[32,8,384]{2,1,0:T(8,128)S(1)}, f32[32,8,384]{2,1,0:T(8,128)}, u32[]{:S(2)}) copy-start(f32[32,8,384]{2,1,0:T(8,128)} %get-tuple-element.25) | copy-start | bytes 1179652
  169.1 1.9 %copy-start.7 = (f32[2,128,384]{2,1,0:T(8,128)S(1)}, f32[2,128,384]{2,1,0:T(8,128)}, u32[]{:S(2)}) copy-start(f32[2,128,384]{2,1,0:T(8,128)} %copy-done.6) | copy-start | bytes 1179652
  169.1 1.9 %copy-start.12 = (f32[2,128,384]{2,1,0:T(8,128)S(1)}, f32[2,128,384]{2,1,0:T(8,128)}, u32[]{:S(2)}) copy-start(f32[2,128,384]{2,1,0:T(8,128)} %param.15) | copy-start | bytes 1179652
  169.1 1.8 %collective-permute-start.4 = (f32[2,128,384]{2,1,0:T(8,128)S(1)}, f32[2,128,384]{2,1,0:T(8,128)S(1)}, u32[]{:S(2)}, u32[]{:S(2)}) collective-permute-start(f32[2,128,384]{2,1,0:T(8,128)S(1)} %dynamic-slice_bitcast_fusion), channel_id=1, source_target_pairs={{0,1},{1,0},{2,3},{3,2},{4,5},{5,4},{6,7},{7,6},{8,9},{9,8},{10,11... | collective-permute-start | bytes 1179656 | tf_op jit(solution)/shard_map/ppermute | solution.py:671

commit v2 on v1

--- a/solution.py
+++ b/solution.py
@@ -12,6 +12,7 @@
 H_FAC = 8
 W_FAC = 6
 ROWS = 4
+PIECE = 32
 
 
 SCALE_NOW = 0.8
@@ -284,73 +285,92 @@
     return (pair[0] * cosine - pair[1] * sine, pair[0] * sine + pair[1] * cosine)
 
 
-def level_out(out_ref, body_rows):
-    values = out_ref[:, :body_rows, :]
-    top = jnp.max(jnp.max(jnp.abs(values), axis=0), axis=0, keepdims=True)
-    top = jnp.maximum(jnp.max(top, axis=1, keepdims=True), 1e-30)
-    power = jnp.ceil(jnp.log2(top)) - 13.0
-    out_ref[:, :body_rows, :] = values * jnp.exp2(-power)
-    tail = out_ref.shape[1] - body_rows
-    out_ref[:, body_rows:, :] = jnp.broadcast_to(
-        power[None], (out_ref.shape[0], tail, out_ref.shape[2])
-    )
-
-
-def columns_kernel(clean_ref, maps_ref, matrix_ref, twiddle_ref, out_ref):
-    coils, _, rows, full = maps_ref.shape
-    groups = out_ref.shape[0]
+def pack(stage_ref, sent_ref, chunk):
+    groups, body, _ = stage_ref.shape
+    planes = body // PIECE
+    tail = sent_ref.shape[2] - body
+
+    def step(g, carry):
+        powers = []
+        for plane in range(planes):
+            spot = slice(plane * PIECE, (plane + 1) * PIECE)
+            values = stage_ref[g, spot, :]
+            top = jnp.maximum(jnp.max(jnp.abs(values), axis=0, keepdims=True), 1e-30)
+            power = jnp.ceil(jnp.log2(top)) - 14.0
+            coded = jnp.round(values * jnp.exp2(-power))
+            sent_ref[chunk, g, spot, :] = coded.astype(jnp.int32).astype(jnp.int16)
+            powers.append(power)
+        powers.append(jnp.zeros((tail - planes, power.shape[1]), jnp.float32))
+        powers = jnp.concatenate(powers, axis=0)
+        sent_ref[chunk, g, body:, :] = powers.astype(jnp.int32).astype(jnp.int16)
+        return carry
+
+    lax.fori_loop(0, groups, step, 0)
+
+
+def unpack(got_ref, chunk, g, first, count, body):
+    powers = got_ref[chunk, g, body:, :].astype(jnp.int32).astype(jnp.float32)
+    scales = jnp.exp2(powers)
+    pieces = []
+    for plane in range(first, first + count):
+        values = got_ref[chunk, g, plane * PIECE : (plane + 1) * PIECE, :]
+        values = values.astype(jnp.int32).astype(jnp.float32)
+        pieces.append(values * scales[plane : plane + 1])
+    return pieces
+
+
+def columns_part(chunk, clean_ref, maps_ref, matrix_ref, twiddle_ref, stage_ref):
+    rows, full = maps_ref.shape[2:]
+    groups = stage_ref.shape[0]
     inner = full // 3
-    piece = inner // groups
     root = math.sqrt(0.75)
     clean = (clean_ref[0], clean_ref[1])
-    for start in range(0, coils, 2):
-        image = [
-            complex_mul((maps_ref[coil, 0], maps_ref[coil, 1]), clean)
-            for coil in (start, start + 1)
-        ]
-        image = [jnp.concatenate([image[0][part], image[1][part]], axis=0) for part in range(2)]
-        first, second, third = [
-            (image[0][:, n * inner : (n + 1) * inner], image[1][:, n * inner : (n + 1) * inner])
-            for n in range(3)
-        ]
-        total = (second[0] + third[0], second[1] + third[1])
-        apart = (root * (second[0] - third[0]), root * (second[1] - third[1]))
-        middle = (first[0] - 0.5 * total[0], first[1] - 0.5 * total[1])
-        bins = (
-            (first[0] + total[0], first[1] + total[1]),
-            (middle[0] + apart[1], middle[1] - apart[0]),
-            (middle[0] - apart[1], middle[1] + apart[0]),
-        )
-        for index in range(3):
-            turned = turn(bins[index], twiddle_ref, index, -1.0)
-            result = lax.dot_general(
-                matrix_ref[...],
-                split_pair(turned[0], turned[1], 1),
-                (((1,), (1,)), ((), ())),
-                preferred_element_type=jnp.float32,
-            )
-            for part in range(2):
-                for which in range(2):
-                    base = ((part * coils + start + which) * 3 + index) * piece
-                    block = result[part * inner : (part + 1) * inner]
-                    block = block[:, which * rows : (which + 1) * rows]
-                    out_ref[:, base : base + piece, :] = block.reshape(groups, piece, rows)
-    level_out(out_ref, 2 * coils * 3 * piece)
-
-
-def rows_kernel(
-    arrived_ref, measured_ref, keep_ref, forward_ref, inverse_ref, twiddle_ref, out_ref
+    image = [
+        complex_mul((maps_ref[coil, 0], maps_ref[coil, 1]), clean)
+        for coil in (2 * chunk, 2 * chunk + 1)
+    ]
+    image = [jnp.concatenate([image[0][part], image[1][part]], axis=0) for part in range(2)]
+    first, second, third = [
+        (image[0][:, n * inner : (n + 1) * inner], image[1][:, n * inner : (n + 1) * inner])
+        for n in range(3)
+    ]
+    total = (second[0] + third[0], second[1] + third[1])
+    apart = (root * (second[0] - third[0]), root * (second[1] - third[1]))
+    middle = (first[0] - 0.5 * total[0], first[1] - 0.5 * total[1])
+    bins = (
+        (first[0] + total[0], first[1] + total[1]),
+        (middle[0] + apart[1], middle[1] - apart[0]),
+        (middle[0] - apart[1], middle[1] + apart[0]),
+    )
+    for index in range(3):
+        turned = turn(bins[index], twiddle_ref, index, -1.0)
+        result = lax.dot_general(
+            matrix_ref[...],
+            split_pair(turned[0], turned[1], 1),
+            (((1,), (1,)), ((), ())),
+            preferred_element_type=jnp.float32,
+        )
+        for part in range(2):
+            for which in range(2):
+                base = ((part * 2 + which) * 3 + index) * PIECE
+                block = result[part * inner : (part + 1) * inner]
+                block = block[:, which * rows : (which + 1) * rows]
+                stage_ref[:, base : base + PIECE, :] = block.reshape(groups, PIECE, rows)
+
+
+def rows_part(
+    chunk, got_ref, targets_ref, keep_ref, permute_ref, forward_ref, inverse_ref, twiddle_ref, stage_ref
 ):
-    groups, _, rows = arrived_ref.shape
-    vectors = measured_ref.shape[1]
+    groups, body, rows = stage_ref.shape
+    vectors = body // 2
+    planes = vectors // PIECE
     height = groups * rows
     inner = height // 4
     copies = vectors // keep_ref.shape[0]
-    scales = [jnp.exp2(arrived_ref[g, 2 * vectors : 2 * vectors + 1, :]) for g in range(groups)]
     whole = [
         jnp.concatenate(
             [
-                arrived_ref[g, part * vectors : (part + 1) * vectors, :] * scales[g]
+                jnp.concatenate(unpack(got_ref, chunk, g, part * planes, planes, body), axis=0)
                 for g in range(groups)
             ],
             axis=1,
@@ -381,8 +401,10 @@
         )
         lanes = slice(index * inner, (index + 1) * inner)
         keep = jnp.concatenate([keep_ref[:, lanes]] * copies, axis=0)
+        spots = slice(chunk * vectors, (chunk + 1) * vectors)
         residual = [
-            keep * (spectrum[:, part * inner : (part + 1) * inner] - measured_ref[part, :, lanes])
+            keep
+            * (spectrum[:, part * inner : (part + 1) * inner] - targets_ref[part, spots, lanes])
             for part in range(2)
         ]
         inverse = jnp.dot(
@@ -406,32 +428,27 @@
     for g in range(groups):
         lanes = slice((g % per_block) * rows, (g % per_block + 1) * rows)
         for part in range(2):
-            out_ref[g, part * vectors : (part + 1) * vectors, :] = blocks[g // per_block][part][
+            stage_ref[g, part * vectors : (part + 1) * vectors, :] = blocks[g // per_block][part][
                 :, lanes
             ]
-    level_out(out_ref, 2 * vectors)
-
-
-def combine_kernel(arrived_ref, maps_ref, matrix_ref, twiddle_ref, *refs):
-    earlier_ref, out_ref = refs if len(refs) == 2 else (None, refs[0])
-    coils, _, rows, full = maps_ref.shape
-    groups = arrived_ref.shape[0]
+
+
+def combine_part(chunk, got_ref, maps_ref, matrix_ref, twiddle_ref, body, out_ref):
+    rows, full = maps_ref.shape[2:]
+    groups = got_ref.shape[1]
     inner = full // 3
-    piece = inner // groups
-    body_rows = 2 * coils * 3 * piece
     root = math.sqrt(0.75)
-    scales = [jnp.exp2(arrived_ref[g, body_rows : body_rows + 1, :]) for g in range(groups)]
 
     def plane(part, coil, index):
-        base = ((part * coils + coil) * 3 + index) * piece
+        spot = (part * 2 + coil) * 3 + index
         return jnp.concatenate(
-            [arrived_ref[g, base : base + piece, :] * scales[g] for g in range(groups)], axis=0
+            [unpack(got_ref, chunk, g, spot, 1, body)[0] for g in range(groups)], axis=0
         )
 
     turned = []
     for index in range(3):
         parts = [
-            jnp.concatenate([plane(part, coil, index) for coil in range(coils)], axis=1)
+            jnp.concatenate([plane(part, coil, index) for coil in range(2)], axis=1)
             for part in range(2)
         ]
         result = lax.dot_general(
@@ -455,53 +472,143 @@
         n, inside = start // inner, slice(start % inner, start % inner + 128)
         lanes = slice(start, start + 128)
         half, place = start // share, slice(start % share, start % share + 128)
-        real = 0.0 if earlier_ref is None else earlier_ref[half, 0, :, place]
-        imag = 0.0 if earlier_ref is None else earlier_ref[half, 1, :, place]
-        for coil in range(coils):
+        real = 0.0 if chunk == 0 else out_ref[half, 0, :, place]
+        imag = 0.0 if chunk == 0 else out_ref[half, 1, :, place]
+        for coil in range(2):
             back = [
                 blocks[n][part][coil * rows : (coil + 1) * rows, inside] for part in range(2)
             ]
-            map_real = maps_ref[coil, 0, :, lanes]
-            map_imag = maps_ref[coil, 1, :, lanes]
+            map_real = maps_ref[2 * chunk + coil, 0, :, lanes]
+            map_imag = maps_ref[2 * chunk + coil, 1, :, lanes]
             real = real + map_real * back[0] + map_imag * back[1]
             imag = imag + map_real * back[1] - map_imag * back[0]
         out_ref[half, 0, :, place] = real
         out_ref[half, 1, :, place] = imag
 
 
-def whole_block(operand):
-    return pl.BlockSpec(operand.shape, lambda i: (0,) * operand.ndim)
-
-
-def part_block(operand, axis, parts, index):
-    block = list(operand.shape)
-    block[axis] //= parts
-    return pl.BlockSpec(
-        tuple(block), lambda i: tuple(index if a == axis else 0 for a in range(operand.ndim))
-    )
-
-
-def call_whole(kernel, shape, name, flops, *operands, specs=None):
-    specs = specs or {}
-    return pl.pallas_call(
-        kernel,
-        grid=(1,),
-        out_shape=jax.ShapeDtypeStruct(shape, jnp.float32),
-        in_specs=[specs.get(i) or whole_block(operand) for i, operand in enumerate(operands)],
-        out_specs=pl.BlockSpec(shape, lambda i: (0,) * len(shape)),
-        compiler_params=pltpu.CompilerParams(vmem_limit_bytes=50 * 1024 * 1024),
-        cost_estimate=pl.CostEstimate(
-            flops=flops, bytes_accessed=8 * math.prod(shape), transcendentals=0
-        ),
-        name=name,
-    )(*operands)
-
-
-def exchange(values):
-    moved = lax.all_to_all(
-        values.astype(jnp.float16), "gz", split_axis=0, concat_axis=0, tiled=True
-    )
-    return moved.astype(jnp.float32)
+def consistency_kernel(
+    clean_ref,
+    maps_ref,
+    left_ref,
+    columns_twiddle_ref,
+    rows_twiddle_ref,
+    sampled_ref,
+    targets_hbm,
+    permute_hbm,
+    forward_hbm,
+    inverse_hbm,
+    right_hbm,
+    out_ref,
+    targets_ref,
+    permute_ref,
+    forward_ref,
+    inverse_ref,
+    right_ref,
+    keep_ref,
+    stage_ref,
+    sent_first,
+    got_first,
+    sent_second,
+    got_second,
+    load_sem,
+    send_sem,
+    recv_sem,
+):
+    groups, body, _ = stage_ref.shape
+    chunks = sent_first.shape[0]
+    me = lax.axis_index("gz")
+    buffers = ((sent_first, got_first), (sent_second, got_second))
+
+    def peer_of(k):
+        return lax.rem(me + k, groups)
+
+    def copy(trip, chunk, target, slot):
+        sent, got = buffers[trip]
+        return pltpu.make_async_remote_copy(
+            src_ref=sent.at[chunk, target],
+            dst_ref=got.at[chunk, slot],
+            send_sem=send_sem.at[trip, chunk, target],
+            recv_sem=recv_sem.at[trip, chunk, slot],
+            device_id={"gz": target},
+            device_id_type=pl.DeviceIdType.MESH,
+        )
+
+    def over_peers(action):
+        def step(k, carry):
+            action(peer_of(k))
+            return carry
+
+        lax.fori_loop(1, groups, step, 0)
+
+    def send(trip, chunk):
+        sent, got = buffers[trip]
+        over_peers(lambda peer: copy(trip, chunk, peer, me).start())
+        got[chunk, me] = sent[chunk, me]
+
+    def receive(trip, chunk):
+        over_peers(lambda peer: copy(trip, chunk, peer, peer).wait_recv())
+
+    barrier = pltpu.get_barrier_semaphore()
+    over_peers(
+        lambda peer: pl.semaphore_signal(
+            barrier, inc=1, device_id={"gz": peer}, device_id_type=pl.DeviceIdType.MESH
+        )
+    )
+    loads = [
+        pltpu.make_async_copy(source, target, load_sem.at[i])
+        for i, (source, target) in enumerate(
+            (
+                (targets_hbm, targets_ref),
+                (permute_hbm, permute_ref),
+                (forward_hbm, forward_ref),
+                (inverse_hbm, inverse_ref),
+                (right_hbm, right_ref),
+            )
+        )
+    ]
+    for load in loads:
+        load.start()
+    for chunk in range(chunks):
+        columns_part(chunk, clean_ref, maps_ref, left_ref, columns_twiddle_ref, stage_ref)
+        pack(stage_ref, sent_first, chunk)
+        if chunk == 0:
+            pl.semaphore_wait(barrier, groups - 1)
+        send(0, chunk)
+    for load in loads:
+        load.wait()
+    keep_ref[...] = jnp.dot(
+        sampled_ref[...], permute_ref[...], preferred_element_type=jnp.float32
+    )
+    for part in range(2):
+        values = targets_ref[part]
+        high = values.astype(jnp.bfloat16)
+        low = (values - high.astype(jnp.float32)).astype(jnp.bfloat16)
+        targets_ref[part] = jnp.dot(
+            high, permute_ref[...], preferred_element_type=jnp.float32
+        ) + jnp.dot(low, permute_ref[...], preferred_element_type=jnp.float32)
+    for chunk in range(chunks):
+        receive(0, chunk)
+        rows_part(
+            chunk,
+            got_first,
+            targets_ref,
+            keep_ref,
+            permute_ref,
+            forward_ref,
+            inverse_ref,
+            rows_twiddle_ref,
+            stage_ref,
+        )
+        pack(stage_ref, sent_second, chunk)
+        send(1, chunk)
+    for chunk in range(chunks):
+        receive(1, chunk)
+        combine_part(
+            chunk, got_second, maps_ref, right_ref, columns_twiddle_ref, body, out_ref
+        )
+    for trip in range(2):
+        for chunk in range(chunks):
+            over_peers(lambda peer: copy(trip, chunk, peer, me).wait_send())
 
 
 def aligned_gradient(clean_wide, coil_maps, measured, sampled):
@@ -509,70 +616,70 @@
     groups = lax.axis_size("gz")
     height = rows * groups
     inner = full // 3
-    piece = inner // groups
-    parts = 2
-    vectors = coils // parts * 3 * piece
-    sent = (groups, 2 * vectors + 16, rows)
-    flops = 12 * vectors * inner * rows * groups
+    chunks = coils // 2
+    body = 2 * 2 * 3 * PIECE
+    halves = lax.axis_size("col")
     high, low = pair_matrix(inner, full, False)
     left = np.concatenate([high, high, low], axis=1)
     right = np.concatenate([high, high, low], axis=0)
-    columns_twiddles = twiddle_rows(3, inner)
     rows_high, rows_low = pair_matrix(height // 4, height, True)
     back_high, back_low = pair_matrix(height // 4, height, False)
     forward = np.concatenate([rows_high, rows_high, rows_low], axis=0)
     inverse = np.concatenate([back_high, back_high, back_low], axis=0)
-    rows_twiddles = twiddle_rows(4, height // 4)
-    spectra = []
-    for part in range(parts):
-        maps = {1: part_block(coil_maps, 0, parts, part)}
-        operands = (clean_wide, coil_maps, left, columns_twiddles)
-        spectra.append(
-            call_whole(columns_kernel, sent, "columns", flops, *operands, specs=maps)
-        )
-        if part == 0:
-            measured, sampled, spectra[0] = lax.optimization_barrier(
-                (measured, sampled, spectra[0])
-            )
-    arrived = [exchange(values) for values in spectra]
-    arrived[0], spectra[1] = lax.optimization_barrier((arrived[0], spectra[1]))
-    place = jnp.arange(height)
+    place = np.arange(height)
     source = place // (height // 4) + 4 * (place % (height // 4))
-    permute = (place[:, None] == source[None, :]).astype(jnp.float32)
-    targets = jnp.transpose(measured.reshape(2, piece, 3, coils, height), (0, 3, 2, 1, 4))
-    targets = jnp.dot(
-        targets.reshape(2 * parts * vectors, height), permute, precision=lax.Precision.HIGH
-    ).reshape(2, parts * vectors, height)
-    keep = jnp.transpose(sampled.reshape(piece, 3, height), (1, 0, 2)).astype(jnp.bfloat16)
-    keep = jnp.dot(
-        keep.reshape(3 * piece, height),
-        permute.astype(jnp.bfloat16),
-        preferred_element_type=jnp.float32,
-    )
-    residual = []
-    for part in range(parts):
-        target = {1: part_block(targets, 1, parts, part)}
-        operands = (arrived[part], targets, keep, forward, inverse, rows_twiddles)
-        residual.append(
-            call_whole(rows_kernel, sent, "rows", 2 * flops, *operands, specs=target)
-        )
-    arrived = [exchange(values) for values in residual]
-    arrived[0], residual[1] = lax.optimization_barrier((arrived[0], residual[1]))
-    halves = lax.axis_size("col")
-    total = ()
-    for part in range(parts):
-        maps = {1: part_block(coil_maps, 0, parts, part)}
-        operands = (arrived[part], coil_maps, right, columns_twiddles) + total
-        shape = (halves, 2, rows, full // halves)
-        total = (call_whole(combine_kernel, shape, "combine", flops, *operands, specs=maps),)
-    return total[0]
+    permute = (place[:, None] == source[None, :]).astype(jnp.bfloat16)
+    targets = jnp.transpose(measured.reshape(2, PIECE, 3, coils, height), (0, 3, 2, 1, 4))
+    targets = targets.reshape(2, coils * 3 * PIECE, height)
+    keep = jnp.transpose(sampled.reshape(PIECE, 3, height), (1, 0, 2)).astype(jnp.bfloat16)
+    keep = keep.reshape(3 * PIECE, height)
+    vmem, anywhere = pl.BlockSpec(memory_space=pltpu.VMEM), pl.BlockSpec(memory_space=pl.ANY)
+    wire = pltpu.VMEM((chunks, groups, body + 16, rows), jnp.int16)
+    return pl.pallas_call(
+        consistency_kernel,
+        out_shape=jax.ShapeDtypeStruct((halves, 2, rows, full // halves), jnp.float32),
+        in_specs=[vmem] * 6 + [anywhere] * 5,
+        out_specs=vmem,
+        scratch_shapes=[
+            pltpu.VMEM(targets.shape, jnp.float32),
+            pltpu.VMEM(permute.shape, jnp.bfloat16),
+            pltpu.VMEM(forward.shape, jnp.bfloat16),
+            pltpu.VMEM(inverse.shape, jnp.bfloat16),
+            pltpu.VMEM(right.shape, jnp.bfloat16),
+            pltpu.VMEM(keep.shape, jnp.float32),
+            pltpu.VMEM((groups, body, rows), jnp.float32),
+            wire,
+            wire,
+            wire,
+            wire,
+            pltpu.SemaphoreType.DMA((5,)),
+            pltpu.SemaphoreType.DMA((2, chunks, groups)),
+            pltpu.SemaphoreType.DMA((2, chunks, groups)),
+        ],
+        compiler_params=pltpu.CompilerParams(
+            vmem_limit_bytes=56 * 1024 * 1024, collective_id=0, has_side_effects=True
+        ),
+        name="consistency",
+    )(
+        clean_wide,
+        coil_maps,
+        left,
+        twiddle_rows(3, inner),
+        twiddle_rows(4, height // 4),
+        keep,
+        targets,
+        permute,
+        forward,
+        inverse,
+        right,
+    )
 
 
 def gradient(clean_wide, coil_maps, measured, sampled):
     coils, _, rows, full = coil_maps.shape
     groups = lax.axis_size("gz")
-    whole = rows % 128 == 0 and coils % 4 == 0 and full % 768 == 0
-    if whole and (rows * groups) % 1024 == 0 and full % (48 * groups) == 0:
+    whole = rows == 128 and coils % 2 == 0 and full == 3 * PIECE * groups
+    if whole and (rows * groups) % 1024 == 0 and full % 768 == 0:
         return aligned_gradient(clean_wide, coil_maps, measured, sampled)
     grad = plain_gradient(clean_wide, coil_maps, measured, sampled)
     return jnp.stack(jnp.split(grad, lax.axis_size("col"), axis=2))

time: 173 us -> 143 us (0.83)
  the two profiles are of different devices: /device:TPU:0 before, /device:TPU:15 now
where the time goes in v2:
time: 143 us
  Pallas kernels  107 us (75%)
  local copies, waits for them, and re-layouts  14.9 us (10%)
  starting transfers between devices  11.6 us (8%)
  other arithmetic  3.97 us (3%)
  blocking collectives  3.44 us (2%)
    pallas_call x1, Pallas kernels, aligned_gradient(): pl.pallas_call(consistency_kernel, out_shape=jax.ShapeDtypeStruct((halves...  81.8 us
    pallas_call x1, Pallas kernels, network(): pl.pallas_call(partial(network_kernel, groups, cols), out_shape=jax.Shape...  25.7 us
    reshape x1, local copies, waits for them, and re-layouts, aligned_gradient(): measured.reshape(2, PIECE, 3, coils, height)  5.35 us
    ppermute x2, starting transfers between devices, with_halo(): lax.ppermute(lax.slice_in_dim(block, block.shape[dim] - width, None, axis...  5.34 us
    ppermute x2, starting transfers between devices, with_halo(): lax.ppermute(lax.slice_in_dim(block, 0, width, axis=dim), axis, backward)  5.28 us
    all_gather x1, blocking collectives, local(): clean_wide = lax.all_gather(clean, 'col', axis=2, tiled=True)  3.44 us
  transfers between devices with their start and end apart: 5, of which 1 were waited for; matrix products, arithmetic and copies ran while one was open for 8% of the time, Pallas kernels for 0%

profile of v2, /device:TPU:15, one launch (start us, length us, event | category | flops | bytes accessed | tf_op | source)
XLA Modules:
  0.0 142.9 jit_solution(14031971701661308652)
XLA Ops:
  0.0 1.1 convert_element_type.81
  1.1 2.1 %collective-permute-start.1 = (bf16[2,3,384]{2,1,0:T(4,128)(2,1)S(1)}, bf16[2,3,384]{2,1,0:T(4,128)(2,1)S(1)}, u32[]{:S(2)}, u32[]{:S(2)}) collective-permute-start(bf16[2,3,384]{2,1,0:T(4,128)(2,1)S(1)} %get-tuple-element.23), channel_id=1, source_target_pairs={{2,0},{4,2},{6,4},{8,6},{10,8},{12,10},{14,12},{3,1},{5,3},{7,5},{... | collective-permute-start | bytes 13832 | tf_op jit(solution)/shard_map/ppermute | solution.py:34
  3.2 4.0 %collective-permute-start = (bf16[2,3,384]{2,1,0:T(4,128)(2,1)S(1)}, bf16[2,3,384]{2,1,0:T(4,128)(2,1)S(1)}, u32[]{:S(2)}, u32[]{:S(2)}) collective-permute-start(bf16[2,3,384]{2,1,0:T(4,128)(2,1)S(1)} %get-tuple-element.22), channel_id=1, source_target_pairs={{0,2},{2,4},{4,6},{6,8},{8,10},{10,12},{12,14},{1,3},{3,5},{5,7},{... | collective-permute-start | bytes 13832 | tf_op jit(solution)/shard_map/ppermute | solution.py:31
  7.3 0.7 broadcast_multiply_fusion.3
  8.5 0.3 pad_bitcast_fusion.3
  8.8 0.3 maximum_bitcast_fusion
  9.3 0.3 reshape.87
  9.8 3.1 %collective-permute-start.3 = (bf16[2,134,3]{2,1,0:T(8,128)(2,1)S(1)}, bf16[2,134,3]{2,1,0:T(8,128)(2,1)S(1)}, u32[]{:S(2)}, u32[]{:S(2)}) collective-permute-start(bf16[2,134,3]{2,1,0:T(8,128)(2,1)S(1)} %get-tuple-element.21), channel_id=1, source_target_pairs={{1,0},{3,2},{5,4},{7,6},{9,8},{11,10},{13,12},{15,14},{17,16},{19,... | collective-permute-start | bytes 4832 | tf_op jit(solution)/shard_map/ppermute | solution.py:34
  12.9 1.3 collective-permute-start.2
  14.2 0.9 copy.103
  15.1 0.7 reshape.88.inner_ref
  16.8 0.8 copy.111
  17.6 5.4 %copy.112 = f32[2,32,3,4,1024]{4,1,2,3,0:T(8,128)} copy(f32[2,32,3,4,1024]{4,3,2,1,0:T(4,128)} %bitcast.93) | data formatting | bytes 6291456 | tf_op jit(solution)/shard_map/reshape | solution.py:632
  23.0 0.2 fusion.10
  23.2 0.2 slice.87
  23.7 0.2 fusion.28
  23.9 0.2 maximum_bitcast_fusion.1
  24.1 0.1 pad_maximum_fusion
  24.2 0.1 fusion.26
  26.3 0.2 pad.113.tiles_ref
  26.6 25.7 %network.1 = f32[32,8,384]{2,1,0:T(8,128)S(1)} custom-call(bf16[9,400,128]{2,1,0:T(8,128)(2,1)S(1)} %pad.113.tiles_ref, bf16[4,128,256]{2,1,0:T(8,128)(2,1)S(1)} %pad.130.first_ref, bf16[3,384,256]{2,1,0:T(8,128)(2,1)S(1)} %reshape.88.inner_ref, bf16[32,384]{1,0:T(8,128)(2,1)S(1)} %pad.139.last_ref, f32[36,1,256]{2,1,0:T(1,128)S(1)} %reshape_reshape.6.first_rows_ref, ...), custom_call_target="tpu_custom_call" | custom-call | tf_op jit(solution)/shard_map/network/pallas_call | solution.py:169
  52.4 0.2 mul.99
  52.8 0.1 mul.101
  52.9 0.5 copy-done.1
  53.4 3.4 %all_gather.3.clean_ref = f32[2,128,768]{2,1,0:T(8,128)} all-gather(f32[2,128,384]{2,1,0:T(8,128)S(1)} %subtract_multiply_fusion), channel_id=1, replica_groups=mesh['grp'=2,'gz'=8,'col'=2] {'col'}, dimensions={2}, use_global_device_ids=true | all-gather | bytes 1179648 | tf_op jit(solution)/shard_map/all_gather | solution.py:772
  56.9 81.8 %consistency.1 = f32[2,2,128,384]{3,2,1,0:T(8,128)} custom-call(f32[2,128,768]{2,1,0:T(8,128)} %all_gather.3.clean_ref, f32[4,2,128,768]{3,2,1,0:T(8,128)} %maps_ref.1, bf16[512,1536]{1,0:T(8,128)(2,1)} %constant.78.clone.left_ref, f32[3,2,256]{2,1,0:T(2,128)} %constant.79.clone.columns_twiddle_ref, f32[4,2,256]{2,1,0:T(2,128)} %constant.80.clone.rows_twiddle_ref, ...), custom_call_target="tpu_custom_call" | custom-call | tf_op jit(solution)/shard_map/consistency/pallas_call | solution.py:638
  138.7 1.0 dynamic-slice_bitcast_fusion
  139.7 0.9 collective-permute-start.4
  140.7 0.2 mul.106
  141.0 0.1 mul.108
  141.2 0.9 collective-permute-done.4
  142.0 0.8 fusion.8
  (93 shorter events, 4.2 us)
Async XLA Ops:
  0.0 8.5 %copy-start.4 = (bf16[1,9,64,64]{3,2,1,0:T(8,128)(2,1)S(1)}, bf16[1,9,64,64]{3,2,1,0:T(8,128)(2,1)}, u32[]{:S(2)}) copy-start(bf16[1,9,64,64]{3,2,1,0:T(8,128)(2,1)} %param.21) | copy-start | bytes 221188
  1.1 7.7 %copy-start.5 = (bf16[9,2,64]{2,1,0:T(2,128)(2,1)S(1)}, bf16[9,2,64]{2,1,0:T(2,128)(2,1)}, u32[]{:S(2)}) copy-start(bf16[9,2,64]{2,1,0:T(2,128)(2,1)} %param.22) | copy-start | bytes 6916
  1.1 8.5 %collective-permute-start.1 = (bf16[2,3,384]{2,1,0:T(4,128)(2,1)S(1)}, bf16[2,3,384]{2,1,0:T(4,128)(2,1)S(1)}, u32[]{:S(2)}, u32[]{:S(2)}) collective-permute-start(bf16[2,3,384]{2,1,0:T(4,128)(2,1)S(1)} %get-tuple-element.23), channel_id=1, source_target_pairs={{2,0},{4,2},{6,4},{8,6},{10,8},{12,10},{14,12},{3,1},{5,3},{7,5},{... | collective-permute-start | bytes 13832 | tf_op jit(solution)/shard_map/ppermute | solution.py:34
  3.2 6.4 %collective-permute-start = (bf16[2,3,384]{2,1,0:T(4,128)(2,1)S(1)}, bf16[2,3,384]{2,1,0:T(4,128)(2,1)S(1)}, u32[]{:S(2)}, u32[]{:S(2)}) collective-permute-start(bf16[2,3,384]{2,1,0:T(4,128)(2,1)S(1)} %get-tuple-element.22), channel_id=1, source_target_pairs={{0,2},{2,4},{4,6},{6,8},{8,10},{10,12},{12,14},{1,3},{3,5},{5,7},{... | collective-permute-start | bytes 13832 | tf_op jit(solution)/shard_map/ppermute | solution.py:31
  9.8 13.2 %collective-permute-start.3 = (bf16[2,134,3]{2,1,0:T(8,128)(2,1)S(1)}, bf16[2,134,3]{2,1,0:T(8,128)(2,1)S(1)}, u32[]{:S(2)}, u32[]{:S(2)}) collective-permute-start(bf16[2,134,3]{2,1,0:T(8,128)(2,1)S(1)} %get-tuple-element.21), channel_id=1, source_target_pairs={{1,0},{3,2},{5,4},{7,6},{9,8},{11,10},{13,12},{15,14},{17,16},{19,... | collective-permute-start | bytes 4832 | tf_op jit(solution)/shard_map/ppermute | solution.py:34
  12.9 10.1 %collective-permute-start.2 = (bf16[2,134,3]{2,1,0:T(8,128)(2,1)S(1)}, bf16[2,134,3]{2,1,0:T(8,128)(2,1)S(1)}, u32[]{:S(2)}, u32[]{:S(2)}) collective-permute-start(bf16[2,134,3]{2,1,0:T(8,128)(2,1)S(1)} %get-tuple-element.20), channel_id=1, source_target_pairs={{0,1},{2,3},{4,5},{6,7},{8,9},{10,11},{12,13},{14,15},{16,17},{18,... | collective-permute-start | bytes 4832 | tf_op jit(solution)/shard_map/ppermute | solution.py:31
  15.1 1.5 %copy-start.3 = (s32[96,1024]{1,0:T(8,128)S(1)}, s32[96,1024]{1,0:T(8,128)}, u32[]{:S(2)}) copy-start(s32[96,1024]{1,0:T(8,128)} %param.19) | copy-start | bytes 1179652
  52.4 1.0 copy-start.1
  139.7 2.3 %collective-permute-start.4 = (f32[2,128,384]{2,1,0:T(8,128)S(1)}, f32[2,128,384]{2,1,0:T(8,128)S(1)}, u32[]{:S(2)}, u32[]{:S(2)}) collective-permute-start(f32[2,128,384]{2,1,0:T(8,128)S(1)} %dynamic-slice_bitcast_fusion), channel_id=1, source_target_pairs={{0,1},{1,0},{2,3},{3,2},{4,5},{5,4},{6,7},{7,6},{8,9},{9,8},{10,11... | collective-permute-start | bytes 1179656 | tf_op jit(solution)/shard_map/ppermute | solution.py:778
  140.7 1.4 copy-start
  140.7 1.4 copy-start.2
